TPU v7x, 512 devices: a whole 4x8x8 slice. The times are simulated.
512 devices in a mesh: row: 16 (over y, core), col: 32 (over z, x).
Axes of the slice: x: 4, y: 8, z: 8, core: 2. Of those that a mesh axis runs over, the one named last changes fastest.
Arguments:
- tokens: bfloat16 [512, 6144], P('col', 'row'), may hold values from -21 to 21
- token_frame: int32 [512], P('col'), may hold values from 0 to 15, never falling along the last dimension, each value on 1 to 64 neighbouring positions
- noise_level: int32 [16], replicated, may hold values from 0 to 63
- modulation: bfloat16 [64, 3, 6144], P(None, None, 'row'), may hold values from -3 to 3
- gate_weight: bfloat16 [6144, 16384], P('row', 'col'), may hold values from -0.078125 to 0.078125
- up_weight: bfloat16 [6144, 16384], P('row', 'col'), may hold values from -0.078125 to 0.078125
- down_weight: bfloat16 [16384, 6144], P('col', 'row'), may hold values from -0.046875 to 0.046875
Outputs:
- mixed: bfloat16 [512, 6144], P('col', 'row')
Inputs may be any that keep to these rules, and one draw needn't show every extreme that they name: token_frame never falls along the tokens.
All inputs are finite; a program needn't handle non-finite values.
Results may differ from a plain program's by a relative error of at most 0.015.
Values may be sent and summed in bfloat16 or wider, within the bound.
A program may use at most 64 MiB of HBM per device.

v0:
```python
import jax
import jax.numpy as jnp
from jax import lax
from jax.sharding import PartitionSpec as P

D = 6144


epsilon = 1e-06


def lookup_mods(frames, noise_level, modulation):
    frame_ids = jnp.arange(noise_level.shape[0], dtype=jnp.int32)
    levels = jnp.sum(
        jnp.where(frames[:, None] == frame_ids[None, :], noise_level[None, :], 0), axis=1
    )
    level_ids = jnp.arange(modulation.shape[0], dtype=jnp.int32)
    onehot = (levels[:, None] == level_ids[None, :]).astype(jnp.bfloat16)
    flat_table = modulation.reshape(modulation.shape[0], -1)
    picked = jnp.dot(onehot, flat_table, preferred_element_type=jnp.float32)
    return picked.reshape(frames.shape[0], 3, modulation.shape[2])


def moment_terms(wide_tokens):
    return (jnp.sum(wide_tokens, axis=1), jnp.sum(wide_tokens * wide_tokens, axis=1))


def normalize(wide_tokens, sums, squares, mods):
    center = sums / D
    spread = squares / D - center * center
    return (
        (wide_tokens - center[:, None]) * lax.rsqrt(spread + epsilon)[:, None] * (1.0 + mods[:, 1])
        + mods[:, 0]
    ).astype(jnp.bfloat16)


def on_device(tokens, token_frame, noise_level, modulation, gate_weight, up_weight, down_weight):
    wide_tokens = tokens.astype(jnp.float32)
    local_mods = lookup_mods(token_frame, noise_level, modulation)
    sums, squares = moment_terms(wide_tokens)
    sums, squares = lax.psum((sums, squares), "row")
    normed = normalize(wide_tokens, sums, squares, local_mods)
    all_rows = lax.all_gather(normed, "col", axis=0, tiled=True)
    summed = lax.psum_scatter(
        jnp.stack(
            [
                jnp.dot(all_rows, gate_weight, preferred_element_type=jnp.float32),
                jnp.dot(all_rows, up_weight, preferred_element_type=jnp.float32),
            ],
            axis=1,
        ).astype(jnp.bfloat16),
        "row",
        scatter_dimension=0,
        tiled=True,
    ).astype(jnp.float32)
    hidden_share = (jax.nn.silu(summed[:, 0]) * summed[:, 1]).astype(jnp.bfloat16)
    partial_value = jnp.dot(
        lax.all_gather(hidden_share, "row", axis=0, tiled=True),
        down_weight,
        preferred_element_type=jnp.float32,
    )
    branch = lax.psum_scatter(
        partial_value.astype(jnp.bfloat16), "col", scatter_dimension=0, tiled=True
    ).astype(jnp.float32)
    return (wide_tokens + local_mods[:, 2] * branch).astype(jnp.bfloat16)


def solution(mesh):
    placed = (
        P("col", "row"),
        P("col"),
        P(),
        P(None, None, "row"),
        P("row", "col"),
        P("row", "col"),
        P("col", "row"),
    )
    return jax.shard_map(
        on_device, mesh=mesh, in_specs=placed, out_specs=P("col", "row"), check_vma=False
    )
```

profile of v0, /device:TPU:1, one launch (start us, length us, event | category | flops | bytes accessed | tf_op | source)
XLA Modules:
  0.0 375.2 jit_solution(10591786860522109972)
XLA Ops:
  6.5 0.0 copy-start
  6.5 0.0 copy-start.4
  6.5 0.0 copy-start.5
  6.5 0.0 reduce-scatter.3.cloned.1.call-start
  6.5 0.9 convert_reduce_fusion
  7.4 0.0 copy-done.4
  7.4 0.0 copy-done.5
  7.4 0.2 select_reduce_fusion
  7.6 29.8 %all-reduce = (f32[16]{0:T(128)S(1)}, f32[16]{0:T(128)S(1)}) all-reduce(f32[16]{0:T(128)S(1)} %get-tuple-element.6, f32[16]{0:T(128)S(1)} %get-tuple-element.5), channel_id=1, replica_groups=mesh['row'=16,'col'=32] {'row'}, use_global_device_ids=true, to_apply=%region_4.5 | all-reduce | flops 32 | bytes 256 | tf_op jit(solution)/shard_map/psum | solution.py:41
  37.4 0.0 copy-start.3
  37.4 1.1 fusion.2
  38.5 0.0 copy-done.3
  38.5 0.1 fusion.10
  38.6 38.7 %all_gather.6 = bf16[512,384]{1,0:T(8,128)(2,1)S(1)} all-gather(bf16[16,384]{1,0:T(8,128)(2,1)S(1)} %fusion.10), channel_id=1, replica_groups=mesh['row'=16,'col'=32] {'col'}, dimensions={0}, use_global_device_ids=true | all-gather | bytes 405504 | tf_op jit(solution)/shard_map/all_gather | solution.py:43
  77.3 0.0 copy-done
  77.3 0.0 copy-start.1
  77.3 0.4 fusion.1
  77.8 0.6 copy-done.1
  78.3 0.4 fusion
  78.8 1.1 pad_maximum_fusion
  79.8 0.0 reduce-scatter.3.cloned.1.call-update
  79.9 0.0 reduce-scatter.5.cloned.1.call-start
  79.9 66.3 %reduce-scatter.3.cloned.1.call-done = bf16[32,2,512]{2,0,1:T(8,128)(2,1)} async-done(((bf16[512,2,512]{2,0,1:T(8,128)(2,1)}), bf16[32,2,512]{2,0,1:T(8,128)(2,1)}) %reduce-scatter.3.cloned.1.call-update) | async-done | bytes 65552 | tf_op jit(solution)/shard_map/reduce_scatter | solution.py:44
  146.2 0.8 convert_element_type.25
  147.0 0.0 copy-start.2
  147.1 18.1 %all_gather.7 = bf16[512,512]{1,0:T(8,128)(2,1)S(1)} all-gather(bf16[32,512]{1,0:T(8,128)(2,1)S(1)} %fusion.6), channel_id=1, replica_groups=mesh['row'=16,'col'=32] {'row'}, dimensions={0}, use_global_device_ids=true | all-gather | bytes 557056 | tf_op jit(solution)/shard_map/all_gather | solution.py:58
  165.2 0.0 copy-done.2
  165.2 1.2 convolution_convert_fusion.2
  166.4 0.0 reduce-scatter.5.cloned.1.call-update
  166.4 200.6 %reduce-scatter.5.cloned.1.call-done = bf16[16,384]{1,0:T(8,128)(2,1)} async-done(((bf16[512,384]{1,0:T(8,128)(2,1)}), bf16[16,384]{1,0:T(8,128)(2,1)}) %reduce-scatter.5.cloned.1.call-update) | async-done | bytes 12304 | tf_op jit(solution)/shard_map/reduce_scatter | solution.py:62
  367.1 1.3 fusion.12
  (2 shorter events, 0.0 us)
Async XLA Ops:
  6.5 70.8 %copy-start = (bf16[384,512]{1,0:T(8,128)(2,1)S(1)}, bf16[384,512]{1,0:T(8,128)(2,1)}, u32[]{:S(2)}) copy-start(bf16[384,512]{1,0:T(8,128)(2,1)} %param.12) | copy-start | bytes 1179652
  6.5 0.9 copy-start.4
  6.5 0.9 copy-start.5
  6.5 139.7 %reduce-scatter.3.cloned.1.call-start = ((), (), s32[]{:S(2)}) async-start(), calls=%async_computation.2 | async-start | bytes 1114112 | tf_op jit(solution)/shard_map/reduce_scatter | solution.py:44
  37.4 1.1 copy-start.3
  77.3 1.0 copy-start.1
  79.9 287.2 %reduce-scatter.5.cloned.1.call-start = ((), (), s32[]{:S(2)}) async-start(), calls=%async_computation.3 | async-start | bytes 405504 | tf_op jit(solution)/shard_map/reduce_scatter | solution.py:62
  147.0 18.2 %copy-start.2 = (bf16[512,384]{1,0:T(8,128)(2,1)S(1)}, bf16[512,384]{1,0:T(8,128)(2,1)}, u32[]{:S(2)}) copy-start(bf16[512,384]{1,0:T(8,128)(2,1)} %param.13) | copy-start | bytes 1179652
Sparse Core Ops, SparseCore 0:
  80.0 66.1 reduce-scatter.2
  166.5 200.4 reduce-scatter.4
where the time goes:
time: 380 us; the launch traced here: 375 us
  waiting for transfers between devices  267 us (70%)
  blocking collectives  86.6 us (23%)
  between operations  13.5 us (4%)
  other arithmetic  4.42 us (1%)
    reduce_scatter x1, waiting for transfers between devices, on_device(): lax.psum_scatter(partial_value.astype(jnp.bfloat16), 'col', scatter_dimen...  201 us
    reduce_scatter x1, waiting for transfers between devices, on_device(): lax.psum_scatter(jnp.stack([jnp.dot(all_rows, gate_weight, preferred_elem...  66.3 us
    all_gather x1, blocking collectives, on_device(): all_rows = lax.all_gather(normed, 'col', axis=0, tiled=True)  38.7 us
    psum x1, blocking collectives, on_device(): sums, squares = lax.psum((sums, squares), 'row')  29.8 us
    all_gather x1, blocking collectives, on_device(): lax.all_gather(hidden_share, 'row', axis=0, tiled=True)  18.1 us
  transfers between devices with their start and end apart: 2, of which 2 were waited for; matrix products, arithmetic and copies ran while one was open for 0% of the time, Pallas kernels for 0%

commit v1 on v0

v1 whole, which is shorter than its diff:
```python
import jax
import jax.numpy as jnp
from jax import lax
from jax.experimental import pallas as pl
from jax.experimental.pallas import tpu as pltpu
from jax.sharding import PartitionSpec as P

D = 6144
EPS = 1e-06
NY, NZ, NX = 8, 8, 4
MESH = pl.DeviceIdType.MESH
F32, BF16 = jnp.float32, jnp.bfloat16


def place(y, core, z, x):
    return (y * 2 + core, z * NX + x)


def pieces(value):
    high = value.astype(BF16).astype(F32)
    rest = value - high
    middle = rest.astype(BF16).astype(F32)
    return high, middle, rest - middle


def in_lanes(lane, first, columns, base):
    for i, column in enumerate(columns):
        base = jnp.where(lane == first + i, column, base)
    return base


def send(src, dst, send_sem, recv_sem, device):
    pltpu.make_async_remote_copy(
        src, dst, send_sem, recv_sem, device_id=device, device_id_type=MESH
    ).start()


def await_bytes(ref, sem):
    pltpu.make_async_copy(ref, ref, sem).wait()


def kernel(
    tokens, frame, noise, modulation, gate_w, up_w, down_w, out,
    own, table, w1, w2, sum_out, sum_in, stat_out, stats, gathered, fields, picks,
    normed, part, part_in, hidden, down, down_in, down_mid, branch_in, own_out,
    local_sem, share_send, share_recv, sum_send, sum_recv, tok_send, tok_recv,
    fwd_send, fwd_recv, stat_send, stat_recv, statf_send, statf_recv, part_send, part_recv, hid_send, hid_recv,
    dx_send, dx_recv, dz_send, dz_recv, stat_recv_own,
):
    row, col = lax.axis_index("row"), lax.axis_index("col")
    y, k, z, x = row // 2, row % 2, col // NX, col % NX
    hz = z // 4
    zz = z % 4
    sibling = place(y, 1 - k, z, x)

    own_copy = pltpu.make_async_copy(tokens, own, local_sem.at[0])
    own_copy.start()
    local = [
        pltpu.make_async_copy(modulation, table.at[k], local_sem.at[1]),
        pltpu.make_async_copy(gate_w, w1.at[pl.ds(384 * k, 384), pl.ds(0, 512)], local_sem.at[2]),
        pltpu.make_async_copy(up_w, w1.at[pl.ds(384 * k, 384), pl.ds(512, 512)], local_sem.at[3]),
        pltpu.make_async_copy(down_w, w2.at[k], local_sem.at[4]),
    ]
    for copy in local:
        copy.start()

    barrier = pltpu.get_barrier_semaphore()
    peers = [place((y + dy) % NY, (k + dk) % 2, z, x) for dy in (4, 3, 5, 2, 6, 1, 7, 0) for dk in (0, 1) if dy or dk]
    peers += [place(y, (k + dk) % 2, (z + dz) % NZ, x) for dz in (4, 3, 5, 2, 6, 1, 7) for dk in (0, 1)]
    peers += [place(y, k, z, (x + dx) % NX) for dx in (2, 1, 3)]
    for peer in peers:
        pl.semaphore_signal(barrier, inc=1, device_id=peer, device_id_type=MESH)

    own_copy.wait()
    wide = own[...].astype(F32)
    lane = lax.broadcasted_iota(jnp.int32, (16, 128), 1)
    sublane = lax.broadcasted_iota(jnp.int32, (16, 128), 0)
    zero = jnp.zeros((16, 128), F32)
    columns = pieces(jnp.sum(wide, axis=1, keepdims=True)) + pieces(jnp.sum(wide * wide, axis=1, keepdims=True))
    sums = in_lanes(lane, 0, columns, zero).astype(BF16)
    sum_out[...] = sums
    sum_in[row] = sums
    onehot = zero
    for t in range(16):
        level = noise[frame[t]]
        onehot = jnp.where((sublane == t) & (lane == level), 1.0, onehot)

    pl.semaphore_wait(barrier, len(peers))

    for dy in (4, 3, 5, 2, 6, 1, 7, 0):
        for dk in (0, 1):
            if dy or dk:
                send(sum_out, sum_in.at[row], sum_send, sum_recv, place((y + dy) % NY, (k + dk) % 2, z, x))
    block = pl.ds(64 * zz + 16 * x, 16)
    for dz in (4, 3, 5, 2, 6, 1, 7):
        send(own, gathered.at[k, block], tok_send, tok_recv.at[zz, k], place(y, hz, (z + dz) % NZ, x))

    @pl.when(k == hz)
    def _():
        pltpu.make_async_copy(own, gathered.at[k, block], tok_recv.at[zz, k]).start()

    @pl.when(k != hz)
    def _():
        send(own, gathered.at[k, block], tok_send, tok_recv.at[zz, k], sibling)

    send(modulation, table.at[k], share_send.at[0], share_recv.at[0], sibling)
    send(gate_w, w1.at[pl.ds(384 * k, 384), pl.ds(0, 512)], share_send.at[1], share_recv.at[1], sibling)
    send(up_w, w1.at[pl.ds(384 * k, 384), pl.ds(512, 512)], share_send.at[2], share_recv.at[2], sibling)
    send(down_w, w2.at[k], share_send.at[3], share_recv.at[3], sibling)

    await_bytes(sum_in.at[pl.ds(0, 15)], sum_recv)
    total = jnp.sum(sum_in[...].astype(F32), axis=0)
    center = jnp.sum(jnp.where(lane < 3, total, 0.0), axis=1, keepdims=True) / D
    square = jnp.sum(jnp.where((lane >= 3) & (lane < 6), total, 0.0), axis=1, keepdims=True) / D
    scale = lax.rsqrt(square - center * center + EPS)
    stat_out[...] = in_lanes(lane, 64, pieces(center) + pieces(scale), onehot).astype(BF16)

    @pl.when(k == hz)
    def _():
        for dz in (4, 3, 5, 2, 6, 1, 7):
            send(stat_out, stats.at[block], stat_send, stat_recv.at[zz], place(y, k, (z + dz) % NZ, x))
        pltpu.make_async_copy(stat_out, stats.at[block], stat_recv.at[zz]).start()

    for i in range(4):
        from_z = (zz + i) % 4
        came = pl.ds(64 * from_z + 16 * x, 16)
        for kk in (0, 1):
            await_bytes(gathered.at[kk, came], tok_recv.at[from_z, kk])
            for dx in (2, 1, 3):
                send(gathered.at[kk, came], gathered.at[kk, came], fwd_send, fwd_recv, place(y, k, z, (x + dx) % NX))

    local[0].wait()
    await_bytes(table.at[0], share_recv.at[0])
    for kk in (0, 1):
        fields[kk, 64:128, :] = jnp.zeros((64, 768), BF16)
        fields[kk, 0:64, 0:384] = table[kk, :, 0, :]
        fields[kk, 0:64, 384:768] = table[kk, :, 1, :]
    gate_mod = jnp.dot(onehot.astype(BF16)[:, 0:64], table[k, :, 2, :], preferred_element_type=F32)
    source = lax.broadcasted_iota(jnp.int32, (128, 256), 0)
    target = lax.broadcasted_iota(jnp.int32, (128, 256), 1)
    picks[...] = jnp.where(
        ((target < 128) & (source >= 64) & (source < 67)) | ((target >= 128) & (source >= 67) & (source < 70)), 1.0, 0.0
    ).astype(BF16)

    for i in range(4):
        from_z = (zz + i) % 4
        came = pl.ds(64 * from_z + 16 * x, 16)
        await_bytes(stats.at[came], stat_recv.at[from_z])
        for dx in (2, 1, 3):
            send(stats.at[came], stats.at[came], statf_send, statf_recv, place(y, k, z, (x + dx) % NX))
    await_bytes(gathered.at[:, pl.ds(0, 192)], fwd_recv)
    await_bytes(stats.at[pl.ds(0, 192)], statf_recv)

    table_of = stats[...]
    moments = jnp.dot(table_of, picks[...], preferred_element_type=F32)
    for kk in (0, 1):
        mods = jnp.dot(table_of, fields[kk], preferred_element_type=F32)
        for part_of in range(3):
            at = slice(128 * part_of, 128 * part_of + 128)
            after = slice(384 + 128 * part_of, 512 + 128 * part_of)
            normed[:, 384 * kk + 128 * part_of : 384 * kk + 128 * part_of + 128] = (
                (gathered[kk, :, at].astype(F32) - moments[:, 0:128]) * moments[:, 128:256] * (1.0 + mods[:, after])
                + mods[:, at]
            ).astype(BF16)

    local[1].wait()
    local[2].wait()
    await_bytes(w1.at[pl.ds(0, 384), pl.ds(0, 512)], share_recv.at[1])
    await_bytes(w1.at[pl.ds(0, 384), pl.ds(0, 512)], share_recv.at[2])
    for n in range(2):
        at = slice(512 * n, 512 * n + 512)
        part[:, at] = jnp.dot(normed[...], w1[:, at], preferred_element_type=F32).astype(BF16)
    for dy in (4, 3, 5, 2, 6, 1, 7):
        to = (y + dy) % NY
        send(part.at[pl.ds(32 * to, 32)], part_in.at[dy - 1], part_send, part_recv, place(to, k, z, x))

    await_bytes(sum_in.at[pl.ds(0, 15)], sum_send)
    await_bytes(gathered.at[0, pl.ds(0, 112)], tok_send)

    @pl.when(k != hz)
    def _():
        await_bytes(own, tok_send)

    @pl.when(k == hz)
    def _():
        await_bytes(stats.at[pl.ds(0, 112)], stat_send)

    await_bytes(gathered.at[:, pl.ds(0, 192)], fwd_send)
    await_bytes(stats.at[pl.ds(0, 192)], statf_send)
    await_bytes(table.at[0], share_send.at[0])
    await_bytes(w1.at[pl.ds(0, 384), pl.ds(0, 512)], share_send.at[1])
    await_bytes(w1.at[pl.ds(0, 384), pl.ds(0, 512)], share_send.at[2])
    await_bytes(w2.at[0], share_send.at[3])
    local[3].wait()
    await_bytes(w2.at[0], share_recv.at[3])

    await_bytes(part_in, part_recv)
    mine = pl.ds(pl.multiple_of(32 * y, 32), 32)
    gate_up = part[mine, :].astype(F32) + jnp.sum(part_in[...].astype(F32), axis=0)
    gate, up = gate_up[:, 0:512], gate_up[:, 512:1024]
    hidden[mine, :] = (gate / (1.0 + jnp.exp(-gate)) * up).astype(BF16)
    for dy in (4, 3, 5, 2, 6, 1, 7):
        send(hidden.at[mine], hidden.at[mine], hid_send, hid_recv, place((y + dy) % NY, k, z, x))
    await_bytes(part_in, part_send)
    await_bytes(hidden.at[pl.ds(0, 224)], hid_recv)

    for kk in (0, 1):
        share = jnp.dot(hidden[...], w2[kk], preferred_element_type=F32).astype(BF16)
        for to_z in range(4):
            for to_x in range(NX):
                at = 64 * to_z + 16 * to_x
                down[to_z, to_x, kk] = share[at : at + 16, :]
    for to_z in range(4):
        for dx in (2, 1, 3):
            to = (x + dx) % NX
            send(down.at[to_z, to], down_in.at[to_z, dx - 1], dx_send, dx_recv.at[to_z], place(y, k, z, to))
    await_bytes(hidden.at[pl.ds(0, 224)], hid_send)
    for to_z in range(4):
        await_bytes(down_in.at[to_z], dx_recv.at[to_z])
        for kk in (0, 1):
            down_mid[to_z, kk] = (
                down[to_z, x, kk].astype(F32) + jnp.sum(down_in[to_z, :, kk].astype(F32), axis=0)
            ).astype(BF16)
        goal = 4 * k + to_z
        for kk in (0, 1):
            here = (goal == z) & (k == kk)

            @pl.when(here)
            def _(to_z=to_z, kk=kk):
                pltpu.make_async_copy(down_mid.at[to_z, kk], branch_in.at[z], dz_recv).start()

            @pl.when(jnp.logical_not(here))
            def _(to_z=to_z, kk=kk, goal=goal):
                send(down_mid.at[to_z, kk], branch_in.at[z], dz_send, dz_recv, place(y, kk, goal, x))

    await_bytes(down_in, dx_send)
    await_bytes(branch_in, dz_recv)
    branch = jnp.sum(branch_in[...].astype(F32), axis=0)
    own_out[...] = (own[...].astype(F32) + gate_mod * branch).astype(BF16)
    result = pltpu.make_async_copy(own_out, out, local_sem.at[5])
    result.start()
    await_bytes(branch_in.at[pl.ds(0, 7)], dz_send)

    @pl.when(k != hz)
    def _():
        await_bytes(own, dz_send)

    result.wait()


def on_device(tokens, token_frame, noise_level, modulation, gate_weight, up_weight, down_weight):
    hbm = pl.BlockSpec(memory_space=pl.ANY)
    smem = pl.BlockSpec(memory_space=pltpu.SMEM)
    vmem, dma = pltpu.VMEM, pltpu.SemaphoreType.DMA
    return pl.pallas_call(
        kernel,
        out_shape=jax.ShapeDtypeStruct((16, 384), BF16),
        in_specs=[hbm, smem, smem, hbm, hbm, hbm, hbm],
        out_specs=hbm,
        scratch_shapes=[
            vmem((16, 384), BF16),
            vmem((2, 64, 3, 384), BF16),
            vmem((768, 1024), BF16),
            vmem((2, 512, 384), BF16),
            vmem((16, 128), BF16),
            vmem((16, 16, 128), BF16),
            vmem((16, 128), BF16),
            vmem((256, 128), BF16),
            vmem((2, 256, 384), BF16),
            vmem((2, 128, 768), BF16),
            vmem((128, 256), BF16),
            vmem((256, 768), BF16),
            vmem((256, 1024), BF16),
            vmem((7, 32, 1024), BF16),
            vmem((256, 512), BF16),
            vmem((4, 4, 2, 16, 384), BF16),
            vmem((4, 3, 2, 16, 384), BF16),
            vmem((4, 2, 16, 384), BF16),
            vmem((8, 16, 384), BF16),
            vmem((16, 384), BF16),
            dma((6,)),
            dma((4,)),
            dma((4,)),
            dma,
            dma,
            dma,
            dma((4, 2)),
            dma,
            dma,
            dma,
            dma((4,)),
            dma,
            dma,
            dma,
            dma,
            dma,
            dma,
            dma,
            dma((4,)),
            dma,
            dma,
            dma,
        ],
        compiler_params=pltpu.CompilerParams(
            collective_id=0, has_side_effects=True, vmem_limit_bytes=48 << 20
        ),
        cost_estimate=pl.CostEstimate(flops=604_000_000, bytes_accessed=1_400_000, transcendentals=16384),
        name="modulated_feed_forward",
    )(tokens, token_frame, noise_level, modulation, gate_weight, up_weight, down_weight)


def solution(mesh):
    placed = (
        P("col", "row"),
        P("col"),
        P(),
        P(None, None, "row"),
        P("row", "col"),
        P("row", "col"),
        P("col", "row"),
    )
    return jax.shard_map(
        on_device, mesh=mesh, in_specs=placed, out_specs=P("col", "row"), check_vma=False
    )
```

time: 380 us -> 64.9 us (0.17); the launches traced: 375 us -> 64.7 us
  waiting for transfers between devices: 267 us -> 0 us
  blocking collectives: 86.6 us -> 0 us
  Pallas kernels: 0 us -> 60 us
  between operations: 13.5 us -> 0.05 us
  other arithmetic: 4.42 us -> 0 us
  local copies, waits for them, and re-layouts: 0.58 us -> 4.67 us
    reduce_scatter x2 -> x0, waiting for transfers between devices: 267 us -> none  [the longest x1 201 us: on_device(): lax.psum_scatter(partial_value.astype(jnp.bfloat16), 'col', scatter_dimen...]
    pallas_call x0 -> x1, Pallas kernels: none -> 60 us  [on_device(): pl.pallas_call(kernel, out_shape=jax.ShapeDtypeStruct((16, 384), BF16), i...]
    all_gather x2 -> x0, blocking collectives: 56.8 us -> none  [the longest x1 38.7 us: on_device(): all_rows = lax.all_gather(normed, 'col', axis=0, tiled=True)]
    psum x1 -> x0, blocking collectives: 29.8 us -> none  [on_device(): sums, squares = lax.psum((sums, squares), 'row')]
    unnamed x12 -> x14, local copies, waits for them, and re-layouts: 0.58 us -> 4.67 us
  transfers between devices with their start and end apart: 2 -> 0, of which waited for: 2 -> 0; matrix products, arithmetic and copies ran while one was open for 0% -> 0% of each run, Pallas kernels for 0% -> 0%
where the time goes in v1:
time: 64.9 us; the launch traced here: 64.7 us
  Pallas kernels  60 us (92%)
  local copies, waits for them, and re-layouts  4.67 us (7%)
    pallas_call x1, Pallas kernels, on_device(): pl.pallas_call(kernel, out_shape=jax.ShapeDtypeStruct((16, 384), BF16), i...  60 us
    unnamed x14, local copies, waits for them, and re-layouts  4.67 us

profile of v1, /device:TPU:1, one launch (start us, length us, event | category | flops | bytes accessed | tf_op | source)
XLA Modules:
  0.0 64.7 jit_solution(7056256293351850164)
XLA Ops:
  0.0 0.0 copy-start.5
  0.0 0.0 copy-start.4
  0.0 0.0 copy-start.3
  0.0 1.1 %copy.8.modulation = bf16[64,3,384]{2,1,0:T(4,128)(2,1)S(1)} copy(bf16[64,3,384]{2,0,1:T(8,128)(2,1)} %param.10) | data formatting | bytes 294912 | tf_op args[3]
  1.1 0.0 copy-done.5
  1.1 0.0 copy-done.4
  1.1 0.0 copy-done.3
  1.1 0.0 copy-start
  1.1 1.0 %copy-done = bf16[384,512]{1,0:T(8,128)(2,1)S(1)} copy-done((bf16[384,512]{1,0:T(8,128)(2,1)S(1)}, bf16[384,512]{1,0:T(8,128)(2,1)}, u32[]{:S(2)}) %copy-start) | copy-done | bytes 393240
  2.1 0.0 copy-start.1
  2.1 1.0 %copy-done.1 = bf16[384,512]{1,0:T(8,128)(2,1)S(1)} copy-done((bf16[384,512]{1,0:T(8,128)(2,1)S(1)}, bf16[384,512]{1,0:T(8,128)(2,1)}, u32[]{:S(2)}) %copy-start.1) | copy-done | bytes 393240
  3.1 0.0 copy-start.2
  3.1 1.0 %copy-done.2 = bf16[512,384]{1,0:T(8,128)(2,1)S(1)} copy-done((bf16[512,384]{1,0:T(8,128)(2,1)S(1)}, bf16[512,384]{1,0:T(8,128)(2,1)}, u32[]{:S(2)}) %copy-start.2) | copy-done | bytes 393240
  4.1 60.0 %modulated_feed_forward.1 = bf16[16,384]{1,0:T(8,128)(2,1)S(1)} custom-call(bf16[16,384]{1,0:T(8,128)(2,1)S(1)} %copy-done.3, s32[16]{0:T(128)S(1)} %copy-done.4, s32[16]{0:T(128)S(1)} %copy-done.5, bf16[64,3,384]{2,1,0:T(4,128)(2,1)S(1)} %copy.8.modulation, bf16[384,512]{1,0:T(8,128)(2,1)S(1)} %copy-done, bf16[384,512]{1,0:T(8,128)(2,1)S(1)} %copy-done.1, ...), custom_call_target="tpu_custom_call" | custom-call | flops 604000000 | bytes 1400000 | tf_op jit(solution)/shard_map/modulated_feed_forward/pallas_call | solution.py:255
  64.1 0.6 copy.10
Async XLA Ops:
  0.0 1.1 %copy-start.5 = (s32[16]{0:T(128)S(1)}, s32[16]{0:T(128)}, u32[]{:S(2)}) copy-start(s32[16]{0:T(128)} %noise.1) | copy-start | bytes 196
  0.0 1.1 %copy-start.4 = (s32[16]{0:T(128)S(1)}, s32[16]{0:T(128)}, u32[]{:S(2)}) copy-start(s32[16]{0:T(128)} %frame.1) | copy-start | bytes 196
  0.0 1.1 %copy-start.3 = (bf16[16,384]{1,0:T(8,128)(2,1)S(1)}, bf16[16,384]{1,0:T(8,128)(2,1)}, u32[]{:S(2)}) copy-start(bf16[16,384]{1,0:T(8,128)(2,1)} %tokens.1) | copy-start | bytes 36868
  1.1 1.0 %copy-start = (bf16[384,512]{1,0:T(8,128)(2,1)S(1)}, bf16[384,512]{1,0:T(8,128)(2,1)}, u32[]{:S(2)}) copy-start(bf16[384,512]{1,0:T(8,128)(2,1)} %gate_w.1) | copy-start | bytes 1179652
  2.1 1.0 %copy-start.1 = (bf16[384,512]{1,0:T(8,128)(2,1)S(1)}, bf16[384,512]{1,0:T(8,128)(2,1)}, u32[]{:S(2)}) copy-start(bf16[384,512]{1,0:T(8,128)(2,1)} %up_w.1) | copy-start | bytes 1179652
  3.1 1.0 %copy-start.2 = (bf16[512,384]{1,0:T(8,128)(2,1)S(1)}, bf16[512,384]{1,0:T(8,128)(2,1)}, u32[]{:S(2)}) copy-start(bf16[512,384]{1,0:T(8,128)(2,1)} %down_w.1) | copy-start | bytes 1179652

commit v2 on v1

--- a/solution.py
+++ b/solution.py
@@ -42,10 +42,10 @@
 def kernel(
     tokens, frame, noise, modulation, gate_w, up_w, down_w, out,
     own, table, w1, w2, sum_out, sum_in, stat_out, stats, gathered, fields, picks,
-    normed, part, part_in, hidden, down, down_in, down_mid, branch_in, own_out,
+    normed, part, part_in, hidden, down, down_in, down_mid, branch_in, levels,
     local_sem, share_send, share_recv, sum_send, sum_recv, tok_send, tok_recv,
     fwd_send, fwd_recv, stat_send, stat_recv, statf_send, statf_recv, part_send, part_recv, hid_send, hid_recv,
-    dx_send, dx_recv, dz_send, dz_recv, stat_recv_own,
+    dx_send, dx_recv, dz_send, dz_recv,
 ):
     row, col = lax.axis_index("row"), lax.axis_index("col")
     y, k, z, x = row // 2, row % 2, col // NX, col % NX
@@ -64,6 +64,13 @@
     for copy in local:
         copy.start()
 
+    small = [
+        pltpu.make_async_copy(frame, levels.at[0], local_sem.at[5]),
+        pltpu.make_async_copy(noise, levels.at[1], local_sem.at[6]),
+    ]
+    for copy in small:
+        copy.start()
+
     barrier = pltpu.get_barrier_semaphore()
     peers = [place((y + dy) % NY, (k + dk) % 2, z, x) for dy in (4, 3, 5, 2, 6, 1, 7, 0) for dk in (0, 1) if dy or dk]
     peers += [place(y, (k + dk) % 2, (z + dz) % NZ, x) for dz in (4, 3, 5, 2, 6, 1, 7) for dk in (0, 1)]
@@ -80,9 +87,11 @@
     sums = in_lanes(lane, 0, columns, zero).astype(BF16)
     sum_out[...] = sums
     sum_in[row] = sums
+    for copy in small:
+        copy.wait()
     onehot = zero
     for t in range(16):
-        level = noise[frame[t]]
+        level = levels[1, levels[0, t]]
         onehot = jnp.where((sublane == t) & (lane == level), 1.0, onehot)
 
     pl.semaphore_wait(barrier, len(peers))
@@ -133,9 +142,9 @@
     await_bytes(table.at[0], share_recv.at[0])
     for kk in (0, 1):
         fields[kk, 64:128, :] = jnp.zeros((64, 768), BF16)
-        fields[kk, 0:64, 0:384] = table[kk, :, 0, :]
-        fields[kk, 0:64, 384:768] = table[kk, :, 1, :]
-    gate_mod = jnp.dot(onehot.astype(BF16)[:, 0:64], table[k, :, 2, :], preferred_element_type=F32)
+        fields[kk, 0:64, 0:384] = table[kk, 0]
+        fields[kk, 0:64, 384:768] = table[kk, 1]
+    gate_mod = jnp.dot(onehot.astype(BF16)[:, 0:64], table[k, 2], preferred_element_type=F32)
     source = lax.broadcasted_iota(jnp.int32, (128, 256), 0)
     target = lax.broadcasted_iota(jnp.int32, (128, 256), 1)
     picks[...] = jnp.where(
@@ -236,30 +245,25 @@
     await_bytes(down_in, dx_send)
     await_bytes(branch_in, dz_recv)
     branch = jnp.sum(branch_in[...].astype(F32), axis=0)
-    own_out[...] = (own[...].astype(F32) + gate_mod * branch).astype(BF16)
-    result = pltpu.make_async_copy(own_out, out, local_sem.at[5])
-    result.start()
+    out[...] = (own[...].astype(F32) + gate_mod * branch).astype(BF16)
     await_bytes(branch_in.at[pl.ds(0, 7)], dz_send)
 
     @pl.when(k != hz)
     def _():
         await_bytes(own, dz_send)
 
-    result.wait()
-
 
 def on_device(tokens, token_frame, noise_level, modulation, gate_weight, up_weight, down_weight):
-    hbm = pl.BlockSpec(memory_space=pl.ANY)
-    smem = pl.BlockSpec(memory_space=pltpu.SMEM)
+    hbm = pl.BlockSpec(memory_space=pltpu.HBM)
     vmem, dma = pltpu.VMEM, pltpu.SemaphoreType.DMA
     return pl.pallas_call(
         kernel,
         out_shape=jax.ShapeDtypeStruct((16, 384), BF16),
-        in_specs=[hbm, smem, smem, hbm, hbm, hbm, hbm],
-        out_specs=hbm,
+        in_specs=[hbm, hbm, hbm, hbm, hbm, hbm, hbm],
+        out_specs=pl.BlockSpec(memory_space=pltpu.VMEM),
         scratch_shapes=[
             vmem((16, 384), BF16),
-            vmem((2, 64, 3, 384), BF16),
+            vmem((2, 3, 64, 384), BF16),
             vmem((768, 1024), BF16),
             vmem((2, 512, 384), BF16),
             vmem((16, 128), BF16),
@@ -277,8 +281,8 @@
             vmem((4, 3, 2, 16, 384), BF16),
             vmem((4, 2, 16, 384), BF16),
             vmem((8, 16, 384), BF16),
-            vmem((16, 384), BF16),
-            dma((6,)),
+            pltpu.SMEM((2, 16), jnp.int32),
+            dma((7,)),
             dma((4,)),
             dma((4,)),
             dma,
@@ -299,14 +303,13 @@
             dma((4,)),
             dma,
             dma,
-            dma,
         ],
         compiler_params=pltpu.CompilerParams(
-            collective_id=0, has_side_effects=True, vmem_limit_bytes=48 << 20
+            collective_id=0, has_side_effects=True, vmem_limit_bytes=60 << 20
         ),
         cost_estimate=pl.CostEstimate(flops=604_000_000, bytes_accessed=1_400_000, transcendentals=16384),
         name="modulated_feed_forward",
-    )(tokens, token_frame, noise_level, modulation, gate_weight, up_weight, down_weight)
+    )(tokens, token_frame, noise_level, jnp.transpose(modulation, (1, 0, 2)), gate_weight, up_weight, down_weight)
 
 
 def solution(mesh):

time: 64.9 us -> 61.2 us (0.943)
  local copies, waits for them, and re-layouts: 4.67 us -> 1.31 us
    unnamed x14 -> x1, local copies, waits for them, and re-layouts: 4.67 us -> 1.31 us
where the time goes in v2:
time: 61.2 us; the launch traced here: 60.9 us
  Pallas kernels  59.6 us (97%)
  local copies, waits for them, and re-layouts  1.31 us (2%)
    pallas_call x1, Pallas kernels, on_device(): pl.pallas_call(kernel, out_shape=jax.ShapeDtypeStruct((16, 384), BF16), i...  59.6 us
    unnamed x1, local copies, waits for them, and re-layouts  1.31 us

profile of v2, /device:TPU:1, one launch (start us, length us, event | category | flops | bytes accessed | tf_op | source)
XLA Modules:
  0.0 60.9 jit_solution(16900942992692149801)
XLA Ops:
  0.0 59.6 %modulated_feed_forward.1 = bf16[16,384]{1,0:T(8,128)(2,1)} custom-call(bf16[16,384]{1,0:T(8,128)(2,1)} %tokens.1, s32[16]{0:T(128)} %frame.1, s32[16]{0:T(128)} %noise.1, bf16[3,64,384]{2,1,0:T(8,128)(2,1)} %bitcast.1, bf16[384,512]{1,0:T(8,128)(2,1)} %gate_w.1, bf16[384,512]{1,0:T(8,128)(2,1)} %up_w.1, bf16[512,384]{1,0:T(8,128)(2,1)} %down_w.1), custom_call_target="tpu_custom_call" | custom-call | flops 604000000 | bytes 1400000 | tf_op jit(solution)/shard_map/modulated_feed_forward/pallas_call | solution.py:259
  59.6 1.3 %copy.9 = bf16[16,384]{1,0:T(8,128)(2,1)} copy(bf16[16,384]{1,0:T(8,128)(2,1)} %modulated_feed_forward.1) | data formatting | bytes 24576

commit v3 on v2

v3 whole, which is shorter than its diff:
```python
import jax
import jax.numpy as jnp
from jax import lax
from jax.experimental import pallas as pl
from jax.experimental.pallas import tpu as pltpu
from jax.sharding import PartitionSpec as P

D = 6144
EPS = 1e-06
NY, NZ, NX = 8, 8, 4
MESH = pl.DeviceIdType.MESH
F32, BF16 = jnp.float32, jnp.bfloat16


def place(y, core, z, x):
    return (y * 2 + core, z * NX + x)


def pieces(value):
    high = value.astype(BF16).astype(F32)
    rest = value - high
    middle = rest.astype(BF16).astype(F32)
    return high, middle, rest - middle


def in_lanes(lane, first, columns, base):
    for i, column in enumerate(columns):
        base = jnp.where(lane == first + i, column, base)
    return base


def send(src, dst, send_sem, recv_sem, device):
    pltpu.make_async_remote_copy(
        src, dst, send_sem, recv_sem, device_id=device, device_id_type=MESH
    ).start()


def await_bytes(ref, sem):
    pltpu.make_async_copy(ref, ref, sem).wait()


class Waits:
    def __init__(self):
        self.owed = {}

    def owe(self, name, ref, sem, when=None):
        self.owed.setdefault(name, []).append((ref, sem, when))

    def take(self, *names):
        for name in names:
            for ref, sem, when in self.owed.pop(name):
                if when is None:
                    await_bytes(ref, sem)
                else:
                    pl.when(when)(lambda ref=ref, sem=sem: await_bytes(ref, sem))


def kernel(
    tokens, frame, noise, modulation, gate_w, up_w, down_w, out,
    own, table, w1, w2, sum_out, sum_in, stat_out, stats, gathered, fields, picks,
    normed, part, part_in, relay, hidden, down, down_in, down_relay, down_mid, branch_in, levels,
    local_sem, share_send, share_recv, sum_send, sum_recv, tok_send, tok_recv,
    fwd_send, fwd_recv, stat_send, stat_recv, statf_send, statf_recv, part_send, part_recv, hid_send, hid_recv,
    dx_send, dx_recv, dz_send, dz_recv,
):
    row, col = lax.axis_index("row"), lax.axis_index("col")
    y, k, z, x = row // 2, row % 2, col // NX, col % NX
    hz = z // 4
    zz = z % 4
    way = 1 - 2 * k
    sibling = place(y, 1 - k, z, x)
    waits = Waits()

    def at_y(step):
        return lax.rem(y + 8 + step * way, NY)

    def at_x(step):
        return lax.rem(x + 4 + step * way, NX)

    def to_y(target):
        return place(target, k, z, x)

    def to_x(target):
        return place(y, k, z, target)

    own_copy = pltpu.make_async_copy(tokens, own, local_sem.at[0])
    own_copy.start()
    small = [
        pltpu.make_async_copy(frame, levels.at[0], local_sem.at[5]),
        pltpu.make_async_copy(noise, levels.at[1], local_sem.at[6]),
    ]
    for copy in small:
        copy.start()
    barrier = pltpu.get_barrier_semaphore()
    peers = [place((y + dy) % NY, (k + dk) % 2, z, x) for dy in (4, 3, 5, 2, 6, 1, 7, 0) for dk in (0, 1) if dy or dk]
    peers += [place(y, (k + dk) % 2, (z + dz) % NZ, x) for dz in (4, 3, 5, 2, 6, 1, 7) for dk in (0, 1)]
    peers += [place(y, k, z, (x + dx) % NX) for dx in (2, 1, 3)]
    for peer in peers:
        pl.semaphore_signal(barrier, inc=1, device_id=peer, device_id_type=MESH)

    own_copy.wait()
    wide = own[...].astype(F32)
    lane = lax.broadcasted_iota(jnp.int32, (16, 128), 1)
    sublane = lax.broadcasted_iota(jnp.int32, (16, 128), 0)
    zero = jnp.zeros((16, 128), F32)
    square = jnp.sum(wide * wide, axis=1, keepdims=True)
    spread_out = jnp.where(lane == sublane, jnp.sum(wide, axis=1, keepdims=True), zero)
    spread_out = jnp.where(lane == sublane + 16, square, spread_out)
    sums = jnp.sum(spread_out, axis=0, keepdims=True)
    sum_out[0] = sums
    sum_in[row] = sums

    pl.semaphore_wait(barrier, len(peers))

    for dy in (4, 3, 5, 2, 6, 1, 7, 0):
        for dk in (0, 1):
            if dy or dk:
                send(sum_out.at[0], sum_in.at[row], sum_send, sum_recv, place((y + dy) % NY, (k + dk) % 2, z, x))
    waits.owe("sum_send", sum_in.at[pl.ds(0, 15)], sum_send)
    waits.owe("sum_recv", sum_in.at[pl.ds(0, 15)], sum_recv)
    block = pl.ds(64 * zz + 16 * x, 16)
    for dz in (4, 3, 5, 2, 6, 1, 7):
        send(own, gathered.at[k, block], tok_send, tok_recv.at[zz, k], place(y, hz, (z + dz) % NZ, x))

    @pl.when(k == hz)
    def _():
        pltpu.make_async_copy(own, gathered.at[k, block], tok_recv.at[zz, k]).start()

    @pl.when(k != hz)
    def _():
        send(own, gathered.at[k, block], tok_send, tok_recv.at[zz, k], sibling)

    waits.owe("tok_send", gathered.at[0, pl.ds(0, 112)], tok_send)
    waits.owe("tok_send", own, tok_send, k != hz)

    half = w1.at[pl.ds(0, 384), pl.ds(0, 512)]
    rows = pl.ds(384 * k, 384)
    for i, (source, goal, like) in enumerate(
        (
            (modulation, table.at[k], table.at[0]),
            (gate_w, w1.at[rows, pl.ds(0, 512)], half),
            (up_w, w1.at[rows, pl.ds(512, 512)], half),
            (down_w, w2.at[k], w2.at[0]),
        )
    ):
        pltpu.make_async_copy(source, goal, local_sem.at[1 + i]).start()
        send(source, goal, share_send.at[i], share_recv.at[i], sibling)
        waits.owe("share_send", like, share_send.at[i])
        waits.owe(("share_recv", i), like, share_recv.at[i])
        waits.owe(("share_recv", i), like, local_sem.at[1 + i])

    for copy in small:
        copy.wait()
    onehot = zero
    for t in range(16):
        level = levels[1, levels[0, t]]
        onehot = jnp.where((sublane == t) & (lane == level), 1.0, onehot)

    waits.take("sum_recv")
    total = jnp.broadcast_to(jnp.sum(sum_in[:, 0, :], axis=0, keepdims=True), (16, 128))
    center = jnp.sum(jnp.where(lane == sublane, total, zero), axis=1, keepdims=True) / D
    square = jnp.sum(jnp.where(lane == sublane + 16, total, zero), axis=1, keepdims=True) / D
    scale = lax.rsqrt(square - center * center + EPS)
    stat_out[...] = in_lanes(lane, 64, pieces(center) + pieces(scale), onehot).astype(BF16)

    @pl.when(k == hz)
    def _():
        for dz in (4, 3, 5, 2, 6, 1, 7):
            send(stat_out, stats.at[block], stat_send, stat_recv.at[zz], place(y, k, (z + dz) % NZ, x))
        pltpu.make_async_copy(stat_out, stats.at[block], stat_recv.at[zz]).start()

    waits.owe("stat_send", stats.at[pl.ds(0, 112)], stat_send, k == hz)

    for i in range(4):
        from_z = (zz + i) % 4
        came = pl.ds(64 * from_z + 16 * x, 16)
        for kk in (0, 1):
            await_bytes(gathered.at[kk, came], tok_recv.at[from_z, kk])
            for dx in (2, 1, 3):
                send(gathered.at[kk, came], gathered.at[kk, came], fwd_send, fwd_recv, to_x((x + dx) % NX))
    waits.owe("fwd_send", gathered.at[:, pl.ds(0, 192)], fwd_send)
    waits.owe("fwd_recv", gathered.at[:, pl.ds(0, 192)], fwd_recv)

    waits.take(("share_recv", 0))
    for kk in (0, 1):
        fields[kk, 64:128, :] = jnp.zeros((64, 768), BF16)
        fields[kk, 0:64, 0:384] = table[kk, 0]
        fields[kk, 0:64, 384:768] = table[kk, 1]
    gate_mod = jnp.dot(onehot.astype(BF16)[:, 0:64], table[k, 2], preferred_element_type=F32)
    source = lax.broadcasted_iota(jnp.int32, (128, 256), 0)
    target = lax.broadcasted_iota(jnp.int32, (128, 256), 1)
    picks[...] = jnp.where(
        ((target < 128) & (source >= 64) & (source < 67)) | ((target >= 128) & (source >= 67) & (source < 70)), 1.0, 0.0
    ).astype(BF16)

    for i in range(4):
        from_z = (zz + i) % 4
        came = pl.ds(64 * from_z + 16 * x, 16)
        await_bytes(stats.at[came], stat_recv.at[from_z])
        for dx in (2, 1, 3):
            send(stats.at[came], stats.at[came], statf_send, statf_recv, to_x((x + dx) % NX))
    waits.owe("statf_send", stats.at[pl.ds(0, 192)], statf_send)
    waits.owe("statf_recv", stats.at[pl.ds(0, 192)], statf_recv)
    waits.take("fwd_recv")
    waits.take("statf_recv")

    table_of = stats[...]
    moments = jnp.dot(table_of, picks[...], preferred_element_type=F32)
    for kk in (0, 1):
        mods = jnp.dot(table_of, fields[kk], preferred_element_type=F32)
        for part_of in range(3):
            at = slice(128 * part_of, 128 * part_of + 128)
            after = slice(384 + 128 * part_of, 512 + 128 * part_of)
            normed[:, 384 * kk + 128 * part_of : 384 * kk + 128 * part_of + 128] = (
                (gathered[kk, :, at].astype(F32) - moments[:, 0:128]) * moments[:, 128:256] * (1.0 + mods[:, after])
                + mods[:, at]
            ).astype(BF16)

    waits.take(("share_recv", 1), ("share_recv", 2))
    for n in range(2):
        at = slice(512 * n, 512 * n + 512)
        part[:, at] = jnp.dot(normed[...], w1[:, at], preferred_element_type=F32).astype(BF16)

    def of_y(target):
        return pl.ds(pl.multiple_of(32 * target, 32), 32)

    for slot, (goal, via) in enumerate(((-4, -2), (-3, -1), (3, 1), (-1, -1), (1, 1))):
        send(part.at[of_y(at_y(goal))], part_in.at[slot], part_send, part_recv.at[slot], to_y(at_y(via)))
        waits.owe(("part", slot), part_in.at[slot], part_recv.at[slot])
    waits.owe("part_send", part_in, part_send)
    waits.take(("part", 2))
    relay[1] = (part[of_y(at_y(2)), :].astype(F32) + part_in[2].astype(F32)).astype(BF16)
    send(relay.at[1], part_in.at[6], part_send, part_recv.at[6], to_y(at_y(2)))
    waits.take(("part", 1), ("part", 0))
    relay[0] = (part[of_y(at_y(-2)), :].astype(F32) + part_in[1].astype(F32) + part_in[0].astype(F32)).astype(BF16)
    send(relay.at[0], part_in.at[5], part_send, part_recv.at[5], to_y(at_y(-2)))
    waits.owe(("part", 5), part_in.at[5], part_recv.at[5])
    waits.owe(("part", 6), part_in.at[6], part_recv.at[6])
    waits.take("sum_send", "tok_send", "fwd_send", "stat_send", "statf_send", "share_send")
    waits.take(("share_recv", 3))
    waits.take(("part", 3), ("part", 4), ("part", 6), ("part", 5))

    mine = of_y(y)
    gate_up = part[mine, :].astype(F32) + jnp.sum(part_in[3:7].astype(F32), axis=0)
    gate, up = gate_up[:, 0:512], gate_up[:, 512:1024]
    hidden[mine, :] = (gate / (1.0 + jnp.exp(-gate)) * up).astype(BF16)
    for slot, step in enumerate((2, -2, 1, -1)):
        send(hidden.at[mine], hidden.at[mine], hid_send, hid_recv.at[min(slot, 2)], to_y(at_y(step)))
    waits.owe("hid_a", hidden.at[pl.ds(0, 32)], hid_recv.at[0])
    waits.owe("hid_b", hidden.at[pl.ds(0, 32)], hid_recv.at[1])
    waits.take("part_send")
    waits.take("hid_a")
    came = of_y(at_y(-2))
    send(hidden.at[came], hidden.at[came], hid_send, hid_recv.at[2], to_y(at_y(2)))
    send(hidden.at[came], hidden.at[came], hid_send, hid_recv.at[2], to_y(at_y(1)))
    waits.take("hid_b")
    came = of_y(at_y(2))
    send(hidden.at[came], hidden.at[came], hid_send, hid_recv.at[2], to_y(at_y(-1)))
    waits.owe("hid_send", hidden.at[pl.ds(0, 224)], hid_send)
    waits.owe("hid_rest", hidden.at[pl.ds(0, 160)], hid_recv.at[2])
    waits.take("hid_rest")

    for kk in (0, 1):
        share = jnp.dot(hidden[...], w2[kk], preferred_element_type=F32).astype(BF16)
        for to_z in range(4):
            for goal_x in range(NX):
                at = 64 * to_z + 16 * goal_x
                down[to_z, goal_x, kk] = share[at : at + 16, :]
    for to_z in range(4):
        send(down.at[to_z, at_x(2)], down_in.at[to_z, 0], dx_send, dx_recv.at[to_z, 0], to_x(at_x(-1)))
    for to_z in range(4):
        send(down.at[to_z, at_x(1)], down_in.at[to_z, 1], dx_send, dx_recv.at[to_z, 1], to_x(at_x(1)))
    waits.take("hid_send")
    for to_z in range(4):
        await_bytes(down_in.at[to_z, 0], dx_recv.at[to_z, 0])
        down_relay[to_z] = (down[to_z, at_x(-1)].astype(F32) + down_in[to_z, 0].astype(F32)).astype(BF16)
        send(down_relay.at[to_z], down_in.at[to_z, 2], dx_send, dx_recv.at[to_z, 2], to_x(at_x(-1)))
    for to_z in range(4):
        await_bytes(down_in.at[to_z, 1], dx_recv.at[to_z, 1])
        await_bytes(down_in.at[to_z, 2], dx_recv.at[to_z, 2])
        down_mid[to_z] = (
            down[to_z, x].astype(F32) + down_in[to_z, 1].astype(F32) + down_in[to_z, 2].astype(F32)
        ).astype(BF16)
        goal = 4 * k + to_z
        for kk in (0, 1):
            here = (goal == z) & (k == kk)

            @pl.when(here)
            def _(to_z=to_z, kk=kk):
                pltpu.make_async_copy(down_mid.at[to_z, kk], branch_in.at[z], dz_recv).start()

            @pl.when(jnp.logical_not(here))
            def _(to_z=to_z, kk=kk, goal=goal):
                send(down_mid.at[to_z, kk], branch_in.at[z], dz_send, dz_recv, place(y, kk, goal, x))

    waits.owe("dx_send", down_in, dx_send)
    waits.owe("dz_recv", branch_in, dz_recv)
    waits.owe("dz_send", branch_in.at[pl.ds(0, 7)], dz_send)
    waits.owe("dz_send", own, dz_send, k != hz)
    waits.take("dz_recv")
    branch = jnp.sum(branch_in[...].astype(F32), axis=0)
    out[...] = (own[...].astype(F32) + gate_mod * branch).astype(BF16)
    waits.take("dx_send", "dz_send")


def on_device(tokens, token_frame, noise_level, modulation, gate_weight, up_weight, down_weight):
    hbm = pl.BlockSpec(memory_space=pltpu.HBM)
    vmem, dma = pltpu.VMEM, pltpu.SemaphoreType.DMA
    return pl.pallas_call(
        kernel,
        out_shape=jax.ShapeDtypeStruct((16, 384), BF16),
        in_specs=[hbm, hbm, hbm, hbm, hbm, hbm, hbm],
        out_specs=pl.BlockSpec(memory_space=pltpu.VMEM),
        scratch_shapes=[
            vmem((16, 384), BF16),
            vmem((2, 3, 64, 384), BF16),
            vmem((768, 1024), BF16),
            vmem((2, 512, 384), BF16),
            vmem((1, 1, 128), F32),
            vmem((16, 1, 128), F32),
            vmem((16, 128), BF16),
            vmem((256, 128), BF16),
            vmem((2, 256, 384), BF16),
            vmem((2, 128, 768), BF16),
            vmem((128, 256), BF16),
            vmem((256, 768), BF16),
            vmem((256, 1024), BF16),
            vmem((7, 32, 1024), BF16),
            vmem((2, 32, 1024), BF16),
            vmem((256, 512), BF16),
            vmem((4, 4, 2, 16, 384), BF16),
            vmem((4, 3, 2, 16, 384), BF16),
            vmem((4, 2, 16, 384), BF16),
            vmem((4, 2, 16, 384), BF16),
            vmem((8, 16, 384), BF16),
            pltpu.SMEM((2, 16), jnp.int32),
            dma((7,)),
            dma((4,)),
            dma((4,)),
            dma,
            dma,
            dma,
            dma((4, 2)),
            dma,
            dma,
            dma,
            dma((4,)),
            dma,
            dma,
            dma,
            dma((7,)),
            dma,
            dma((3,)),
            dma,
            dma((4, 3)),
            dma,
            dma,
        ],
        compiler_params=pltpu.CompilerParams(
            collective_id=0, has_side_effects=True, vmem_limit_bytes=60 << 20
        ),
        cost_estimate=pl.CostEstimate(flops=604_000_000, bytes_accessed=1_400_000, transcendentals=16384),
        name="modulated_feed_forward",
    )(tokens, token_frame, noise_level, jnp.transpose(modulation, (1, 0, 2)), gate_weight, up_weight, down_weight)


def solution(mesh):
    placed = (
        P("col", "row"),
        P("col"),
        P(),
        P(None, None, "row"),
        P("row", "col"),
        P("row", "col"),
        P("col", "row"),
    )
    return jax.shard_map(
        on_device, mesh=mesh, in_specs=placed, out_specs=P("col", "row"), check_vma=False
    )
```

time: 61.2 us -> 60.5 us (0.989)
    pallas_call x1, Pallas kernels: 59.6 us -> 59 us  [on_device(): pl.pallas_call(kernel, out_shape=jax.ShapeDtypeStruct((16, 384), BF16), i...]
where the time goes in v3:
time: 60.5 us; the launch traced here: 60.3 us
  Pallas kernels  59 us (98%)
  local copies, waits for them, and re-layouts  1.31 us (2%)
    pallas_call x1, Pallas kernels, on_device(): pl.pallas_call(kernel, out_shape=jax.ShapeDtypeStruct((16, 384), BF16), i...  59 us
    unnamed x1, local copies, waits for them, and re-layouts  1.31 us

profile of v3, /device:TPU:1, one launch (start us, length us, event | category | flops | bytes accessed | tf_op | source)
XLA Modules:
  0.0 60.3 jit_solution(13792014076314961464)
XLA Ops:
  0.0 59.0 %modulated_feed_forward.1 = bf16[16,384]{1,0:T(8,128)(2,1)} custom-call(bf16[16,384]{1,0:T(8,128)(2,1)} %tokens.1, s32[16]{0:T(128)} %frame.1, s32[16]{0:T(128)} %noise.1, bf16[3,64,384]{2,1,0:T(8,128)(2,1)} %bitcast.1, bf16[384,512]{1,0:T(8,128)(2,1)} %gate_w.1, bf16[384,512]{1,0:T(8,128)(2,1)} %up_w.1, bf16[512,384]{1,0:T(8,128)(2,1)} %down_w.1), custom_call_target="tpu_custom_call" | custom-call | flops 604000000 | bytes 1400000 | tf_op jit(solution)/shard_map/modulated_feed_forward/pallas_call | solution.py:309
  59.0 1.3 %copy.9 = bf16[16,384]{1,0:T(8,128)(2,1)} copy(bf16[16,384]{1,0:T(8,128)(2,1)} %modulated_feed_forward.1) | data formatting | bytes 24576

commit v4 on v3

--- a/solution.py
+++ b/solution.py
@@ -60,7 +60,7 @@
     own, table, w1, w2, sum_out, sum_in, stat_out, stats, gathered, fields, picks,
     normed, part, part_in, relay, hidden, down, down_in, down_relay, down_mid, branch_in, levels,
     local_sem, share_send, share_recv, sum_send, sum_recv, tok_send, tok_recv,
-    fwd_send, fwd_recv, stat_send, stat_recv, statf_send, statf_recv, part_send, part_recv, hid_send, hid_recv,
+    fwd_send, fwd_recv, stat_send, stat_recv, part_send, part_recv, hid_send, hid_recv,
     dx_send, dx_recv, dz_send, dz_recv,
 ):
     row, col = lax.axis_index("row"), lax.axis_index("col")
@@ -83,6 +83,15 @@
     def to_x(target):
         return place(y, k, z, target)
 
+    upper = zz // 2
+    outward = [zz, 1 - zz + 4 * upper, 2 - upper, 3 - 3 * upper]
+    holds = 1 - (k - hz) * (k - hz)
+    near_first = [outward[i] * holds + outward[3 - i] * (1 - holds) for i in range(4)]
+    around_z = {dz: lax.rem(z + dz, NZ) for dz in range(1, NZ)}
+    around_y = {dy: lax.rem(y + dy, NY) for dy in range(NY)}
+    around_x = {dx: lax.rem(x + dx, NX) for dx in range(1, NX)}
+    far_z, far_y = (4, 3, 5, 2, 6, 1, 7), (4, 3, 5, 2, 6, 1, 7, 0)
+
     own_copy = pltpu.make_async_copy(tokens, own, local_sem.at[0])
     own_copy.start()
     small = [
@@ -92,11 +101,18 @@
     for copy in small:
         copy.start()
     barrier = pltpu.get_barrier_semaphore()
-    peers = [place((y + dy) % NY, (k + dk) % 2, z, x) for dy in (4, 3, 5, 2, 6, 1, 7, 0) for dk in (0, 1) if dy or dk]
-    peers += [place(y, (k + dk) % 2, (z + dz) % NZ, x) for dz in (4, 3, 5, 2, 6, 1, 7) for dk in (0, 1)]
-    peers += [place(y, k, z, (x + dx) % NX) for dx in (2, 1, 3)]
+    peers = [place(y, core, around_z[dz], x) for dz in far_z for core in (k, 1 - k)]
+    peers += [place(around_y[dy], core, z, x) for dy in far_y for core in (k, 1 - k)][:-2] + [sibling]
+    peers += [to_x(around_x[dx]) for dx in (2, 1, 3)]
     for peer in peers:
         pl.semaphore_signal(barrier, inc=1, device_id=peer, device_id_type=MESH)
+    for i in range(4):
+        from_z = 4 * k + i
+
+        @pl.when(from_z != z)
+        def _(from_z=from_z):
+            for dx in (2, 1, 3):
+                pl.semaphore_signal(barrier, inc=1, device_id=place(y, k, from_z, around_x[dx]), device_id_type=MESH)
 
     own_copy.wait()
     wide = own[...].astype(F32)
@@ -110,17 +126,11 @@
     sum_out[0] = sums
     sum_in[row] = sums
 
-    pl.semaphore_wait(barrier, len(peers))
-
-    for dy in (4, 3, 5, 2, 6, 1, 7, 0):
-        for dk in (0, 1):
-            if dy or dk:
-                send(sum_out.at[0], sum_in.at[row], sum_send, sum_recv, place((y + dy) % NY, (k + dk) % 2, z, x))
-    waits.owe("sum_send", sum_in.at[pl.ds(0, 15)], sum_send)
-    waits.owe("sum_recv", sum_in.at[pl.ds(0, 15)], sum_recv)
+    pl.semaphore_wait(barrier, len(peers) + 21 * holds)
+
     block = pl.ds(64 * zz + 16 * x, 16)
     for dz in (4, 3, 5, 2, 6, 1, 7):
-        send(own, gathered.at[k, block], tok_send, tok_recv.at[zz, k], place(y, hz, (z + dz) % NZ, x))
+        send(own, gathered.at[k, block], tok_send, tok_recv.at[zz, k], place(y, hz, around_z[dz], x))
 
     @pl.when(k == hz)
     def _():
@@ -132,6 +142,12 @@
 
     waits.owe("tok_send", gathered.at[0, pl.ds(0, 112)], tok_send)
     waits.owe("tok_send", own, tok_send, k != hz)
+
+    for dy in far_y:
+        for core in (k, 1 - k) if dy else (1 - k,):
+            send(sum_out.at[0], sum_in.at[row], sum_send, sum_recv, place(around_y[dy], core, z, x))
+    waits.owe("sum_send", sum_in.at[pl.ds(0, 15)], sum_send)
+    waits.owe("sum_recv", sum_in.at[pl.ds(0, 15)], sum_recv)
 
     half = w1.at[pl.ds(0, 384), pl.ds(0, 512)]
     rows = pl.ds(384 * k, 384)
@@ -165,19 +181,23 @@
 
     @pl.when(k == hz)
     def _():
-        for dz in (4, 3, 5, 2, 6, 1, 7):
-            send(stat_out, stats.at[block], stat_send, stat_recv.at[zz], place(y, k, (z + dz) % NZ, x))
-        pltpu.make_async_copy(stat_out, stats.at[block], stat_recv.at[zz]).start()
-
-    waits.owe("stat_send", stats.at[pl.ds(0, 112)], stat_send, k == hz)
-
-    for i in range(4):
-        from_z = (zz + i) % 4
+        for dz in far_z:
+            for to in (around_x[2], around_x[1], around_x[3], x):
+                send(stat_out, stats.at[block], stat_send, stat_recv, place(y, k, around_z[dz], to))
+        for dx in (2, 1, 3):
+            send(stat_out, stats.at[block], stat_send, stat_recv, to_x(around_x[dx]))
+        pltpu.make_async_copy(stat_out, stats.at[block], stat_recv).start()
+
+    waits.owe("stat_send", stats.at[pl.ds(0, 240)], stat_send, k == hz)
+    waits.owe("stat_send", stats, stat_send, k == hz)
+    waits.owe("stat_recv", stats, stat_recv)
+
+    for from_z in near_first:
         came = pl.ds(64 * from_z + 16 * x, 16)
         for kk in (0, 1):
             await_bytes(gathered.at[kk, came], tok_recv.at[from_z, kk])
             for dx in (2, 1, 3):
-                send(gathered.at[kk, came], gathered.at[kk, came], fwd_send, fwd_recv, to_x((x + dx) % NX))
+                send(gathered.at[kk, came], gathered.at[kk, came], fwd_send, fwd_recv, to_x(around_x[dx]))
     waits.owe("fwd_send", gathered.at[:, pl.ds(0, 192)], fwd_send)
     waits.owe("fwd_recv", gathered.at[:, pl.ds(0, 192)], fwd_recv)
 
@@ -193,16 +213,8 @@
         ((target < 128) & (source >= 64) & (source < 67)) | ((target >= 128) & (source >= 67) & (source < 70)), 1.0, 0.0
     ).astype(BF16)
 
-    for i in range(4):
-        from_z = (zz + i) % 4
-        came = pl.ds(64 * from_z + 16 * x, 16)
-        await_bytes(stats.at[came], stat_recv.at[from_z])
-        for dx in (2, 1, 3):
-            send(stats.at[came], stats.at[came], statf_send, statf_recv, to_x((x + dx) % NX))
-    waits.owe("statf_send", stats.at[pl.ds(0, 192)], statf_send)
-    waits.owe("statf_recv", stats.at[pl.ds(0, 192)], statf_recv)
     waits.take("fwd_recv")
-    waits.take("statf_recv")
+    waits.take("stat_recv")
 
     table_of = stats[...]
     moments = jnp.dot(table_of, picks[...], preferred_element_type=F32)
@@ -216,33 +228,44 @@
                 + mods[:, at]
             ).astype(BF16)
 
-    waits.take(("share_recv", 1), ("share_recv", 2))
-    for n in range(2):
-        at = slice(512 * n, 512 * n + 512)
-        part[:, at] = jnp.dot(normed[...], w1[:, at], preferred_element_type=F32).astype(BF16)
-
     def of_y(target):
         return pl.ds(pl.multiple_of(32 * target, 32), 32)
 
-    for slot, (goal, via) in enumerate(((-4, -2), (-3, -1), (3, 1), (-1, -1), (1, 1))):
-        send(part.at[of_y(at_y(goal))], part_in.at[slot], part_send, part_recv.at[slot], to_y(at_y(via)))
-        waits.owe(("part", slot), part_in.at[slot], part_recv.at[slot])
+    routes = ((-4, -2), (-3, -1), (3, 1), (-1, -1), (1, 1))
+
+    def send_part(n, slot):
+        goal, via = routes[slot]
+        send(part.at[n, of_y(at_y(goal))], part_in.at[n, slot], part_send, part_recv.at[n, slot], to_y(at_y(via)))
+        waits.owe(("part", n, slot), part_in.at[n, slot], part_recv.at[n, slot])
+
+    for n in range(2):
+        waits.take(("share_recv", 1 + n))
+        at = slice(512 * n, 512 * n + 512)
+        part[n] = jnp.dot(normed[...], w1[:, at], preferred_element_type=F32).astype(BF16)
+        for slot in (0, 1, 2):
+            send_part(n, slot)
+    for n in range(2):
+        for slot in (3, 4):
+            send_part(n, slot)
+    for n in range(2):
+        waits.take(("part", n, 2))
+        relay[n, 1] = (part[n, of_y(at_y(2)), :].astype(F32) + part_in[n, 2].astype(F32)).astype(BF16)
+        send(relay.at[n, 1], part_in.at[n, 6], part_send, part_recv.at[n, 6], to_y(at_y(2)))
+        waits.take(("part", n, 1), ("part", n, 0))
+        relay[n, 0] = (
+            part[n, of_y(at_y(-2)), :].astype(F32) + part_in[n, 1].astype(F32) + part_in[n, 0].astype(F32)
+        ).astype(BF16)
+        send(relay.at[n, 0], part_in.at[n, 5], part_send, part_recv.at[n, 5], to_y(at_y(-2)))
+        waits.owe(("part", n, 5), part_in.at[n, 5], part_recv.at[n, 5])
+        waits.owe(("part", n, 6), part_in.at[n, 6], part_recv.at[n, 6])
     waits.owe("part_send", part_in, part_send)
-    waits.take(("part", 2))
-    relay[1] = (part[of_y(at_y(2)), :].astype(F32) + part_in[2].astype(F32)).astype(BF16)
-    send(relay.at[1], part_in.at[6], part_send, part_recv.at[6], to_y(at_y(2)))
-    waits.take(("part", 1), ("part", 0))
-    relay[0] = (part[of_y(at_y(-2)), :].astype(F32) + part_in[1].astype(F32) + part_in[0].astype(F32)).astype(BF16)
-    send(relay.at[0], part_in.at[5], part_send, part_recv.at[5], to_y(at_y(-2)))
-    waits.owe(("part", 5), part_in.at[5], part_recv.at[5])
-    waits.owe(("part", 6), part_in.at[6], part_recv.at[6])
-    waits.take("sum_send", "tok_send", "fwd_send", "stat_send", "statf_send", "share_send")
+    waits.take("sum_send", "tok_send", "fwd_send", "stat_send", "share_send")
     waits.take(("share_recv", 3))
-    waits.take(("part", 3), ("part", 4), ("part", 6), ("part", 5))
+    for n in range(2):
+        waits.take(("part", n, 3), ("part", n, 4), ("part", n, 6), ("part", n, 5))
 
     mine = of_y(y)
-    gate_up = part[mine, :].astype(F32) + jnp.sum(part_in[3:7].astype(F32), axis=0)
-    gate, up = gate_up[:, 0:512], gate_up[:, 512:1024]
+    gate, up = (part[n, mine, :].astype(F32) + jnp.sum(part_in[n, 3:7].astype(F32), axis=0) for n in range(2))
     hidden[mine, :] = (gate / (1.0 + jnp.exp(-gate)) * up).astype(BF16)
     for slot, step in enumerate((2, -2, 1, -1)):
         send(hidden.at[mine], hidden.at[mine], hid_send, hid_recv.at[min(slot, 2)], to_y(at_y(step)))
@@ -266,32 +289,32 @@
             for goal_x in range(NX):
                 at = 64 * to_z + 16 * goal_x
                 down[to_z, goal_x, kk] = share[at : at + 16, :]
-    for to_z in range(4):
-        send(down.at[to_z, at_x(2)], down_in.at[to_z, 0], dx_send, dx_recv.at[to_z, 0], to_x(at_x(-1)))
-    for to_z in range(4):
-        send(down.at[to_z, at_x(1)], down_in.at[to_z, 1], dx_send, dx_recv.at[to_z, 1], to_x(at_x(1)))
+    far_first = near_first[::-1]
+    for i, to_z in enumerate(far_first):
+        send(down.at[to_z, at_x(2)], down_in.at[i, 0], dx_send, dx_recv.at[i, 0], to_x(at_x(-1)))
+        send(down.at[to_z, at_x(1)], down_in.at[i, 1], dx_send, dx_recv.at[i, 1], to_x(at_x(1)))
     waits.take("hid_send")
-    for to_z in range(4):
-        await_bytes(down_in.at[to_z, 0], dx_recv.at[to_z, 0])
-        down_relay[to_z] = (down[to_z, at_x(-1)].astype(F32) + down_in[to_z, 0].astype(F32)).astype(BF16)
-        send(down_relay.at[to_z], down_in.at[to_z, 2], dx_send, dx_recv.at[to_z, 2], to_x(at_x(-1)))
-    for to_z in range(4):
-        await_bytes(down_in.at[to_z, 1], dx_recv.at[to_z, 1])
-        await_bytes(down_in.at[to_z, 2], dx_recv.at[to_z, 2])
-        down_mid[to_z] = (
-            down[to_z, x].astype(F32) + down_in[to_z, 1].astype(F32) + down_in[to_z, 2].astype(F32)
-        ).astype(BF16)
-        goal = 4 * k + to_z
-        for kk in (0, 1):
-            here = (goal == z) & (k == kk)
-
-            @pl.when(here)
-            def _(to_z=to_z, kk=kk):
-                pltpu.make_async_copy(down_mid.at[to_z, kk], branch_in.at[z], dz_recv).start()
-
-            @pl.when(jnp.logical_not(here))
-            def _(to_z=to_z, kk=kk, goal=goal):
-                send(down_mid.at[to_z, kk], branch_in.at[z], dz_send, dz_recv, place(y, kk, goal, x))
+    for i, to_z in enumerate(far_first):
+        await_bytes(down_in.at[i, 0], dx_recv.at[i, 0])
+        down_relay[i] = (down[to_z, at_x(-1)].astype(F32) + down_in[i, 0].astype(F32)).astype(BF16)
+        send(down_relay.at[i], down_in.at[i, 2], dx_send, dx_recv.at[i, 2], to_x(at_x(-1)))
+    for i, to_z in enumerate(far_first):
+        await_bytes(down_in.at[i, 1], dx_recv.at[i, 1])
+        await_bytes(down_in.at[i, 2], dx_recv.at[i, 2])
+        down_mid[i] = (down[to_z, x].astype(F32) + down_in[i, 1].astype(F32) + down_in[i, 2].astype(F32)).astype(BF16)
+        if i < 3:
+            for core in (0, 1):
+                send(down_mid.at[i, core], branch_in.at[z], dz_send, dz_recv, place(y, core, 4 * k + to_z, x))
+
+    send(down_mid.at[3, 1 - k], branch_in.at[z], dz_send, dz_recv, place(y, 1 - k, 4 * k + far_first[3], x))
+
+    @pl.when(k == hz)
+    def _():
+        pltpu.make_async_copy(down_mid.at[3, k], branch_in.at[z], dz_recv).start()
+
+    @pl.when(k != hz)
+    def _():
+        send(down_mid.at[3, k], branch_in.at[z], dz_send, dz_recv, place(y, k, 4 * k + far_first[3], x))
 
     waits.owe("dx_send", down_in, dx_send)
     waits.owe("dz_recv", branch_in, dz_recv)
@@ -324,9 +347,9 @@
             vmem((2, 128, 768), BF16),
             vmem((128, 256), BF16),
             vmem((256, 768), BF16),
-            vmem((256, 1024), BF16),
-            vmem((7, 32, 1024), BF16),
-            vmem((2, 32, 1024), BF16),
+            vmem((2, 256, 512), BF16),
+            vmem((2, 7, 32, 512), BF16),
+            vmem((2, 2, 32, 512), BF16),
             vmem((256, 512), BF16),
             vmem((4, 4, 2, 16, 384), BF16),
             vmem((4, 3, 2, 16, 384), BF16),
@@ -344,11 +367,9 @@
             dma,
             dma,
             dma,
-            dma((4,)),
-            dma,
-            dma,
-            dma,
-            dma((7,)),
+            dma,
+            dma,
+            dma((2, 7)),
             dma,
             dma((3,)),
             dma,

time: 60.5 us -> 60.9 us (level)
  no operation moved by 1% of the time
where the time goes in v4:
time: 60.9 us; the launch traced here: 60.6 us
  Pallas kernels  59.3 us (97%)
  local copies, waits for them, and re-layouts  1.31 us (2%)
    pallas_call x1, Pallas kernels, on_device(): pl.pallas_call(kernel, out_shape=jax.ShapeDtypeStruct((16, 384), BF16), i...  59.3 us
    unnamed x1, local copies, waits for them, and re-layouts  1.31 us

profile of v4, /device:TPU:1, one launch (start us, length us, event | category | flops | bytes accessed | tf_op | source)
XLA Modules:
  0.0 60.6 jit_solution(9076524815541077913)
XLA Ops:
  0.0 59.3 %modulated_feed_forward.1 = bf16[16,384]{1,0:T(8,128)(2,1)} custom-call(bf16[16,384]{1,0:T(8,128)(2,1)} %tokens.1, s32[16]{0:T(128)} %frame.1, s32[16]{0:T(128)} %noise.1, bf16[3,64,384]{2,1,0:T(8,128)(2,1)} %bitcast.1, bf16[384,512]{1,0:T(8,128)(2,1)} %gate_w.1, bf16[384,512]{1,0:T(8,128)(2,1)} %up_w.1, bf16[512,384]{1,0:T(8,128)(2,1)} %down_w.1), custom_call_target="tpu_custom_call" | custom-call | flops 604000000 | bytes 1400000 | tf_op jit(solution)/shard_map/modulated_feed_forward/pallas_call | solution.py:332
  59.3 1.3 %copy.9 = bf16[16,384]{1,0:T(8,128)(2,1)} copy(bf16[16,384]{1,0:T(8,128)(2,1)} %modulated_feed_forward.1) | data formatting | bytes 24576

commit v5 on v4

--- a/solution.py
+++ b/solution.py
@@ -58,7 +58,7 @@
 def kernel(
     tokens, frame, noise, modulation, gate_w, up_w, down_w, out,
     own, table, w1, w2, sum_out, sum_in, stat_out, stats, gathered, fields, picks,
-    normed, part, part_in, relay, hidden, down, down_in, down_relay, down_mid, branch_in, levels,
+    normed, part, part_in, relay, hidden, down, down_in, down_mid, branch_in, levels,
     local_sem, share_send, share_recv, sum_send, sum_recv, tok_send, tok_recv,
     fwd_send, fwd_recv, stat_send, stat_recv, part_send, part_recv, hid_send, hid_recv,
     dx_send, dx_recv, dz_send, dz_recv,
@@ -71,11 +71,8 @@
     sibling = place(y, 1 - k, z, x)
     waits = Waits()
 
-    def at_y(step):
-        return lax.rem(y + 8 + step * way, NY)
-
-    def at_x(step):
-        return lax.rem(x + 4 + step * way, NX)
+    def at_y(step, chunk):
+        return lax.rem(y + 8 + (step if chunk == 0 else -step) * way, NY)
 
     def to_y(target):
         return place(target, k, z, x)
@@ -183,23 +180,25 @@
     def _():
         for dz in far_z:
             for to in (around_x[2], around_x[1], around_x[3], x):
-                send(stat_out, stats.at[block], stat_send, stat_recv, place(y, k, around_z[dz], to))
+                send(stat_out, stats.at[block], stat_send, stat_recv.at[zz], place(y, k, around_z[dz], to))
         for dx in (2, 1, 3):
-            send(stat_out, stats.at[block], stat_send, stat_recv, to_x(around_x[dx]))
-        pltpu.make_async_copy(stat_out, stats.at[block], stat_recv).start()
+            send(stat_out, stats.at[block], stat_send, stat_recv.at[zz], to_x(around_x[dx]))
+        pltpu.make_async_copy(stat_out, stats.at[block], stat_recv.at[zz]).start()
 
     waits.owe("stat_send", stats.at[pl.ds(0, 240)], stat_send, k == hz)
     waits.owe("stat_send", stats, stat_send, k == hz)
-    waits.owe("stat_recv", stats, stat_recv)
+    for i in range(4):
+        waits.owe(("stat_recv", i), stats.at[pl.ds(0, 64)], stat_recv.at[near_first[i]])
 
     for from_z in near_first:
         came = pl.ds(64 * from_z + 16 * x, 16)
         for kk in (0, 1):
             await_bytes(gathered.at[kk, came], tok_recv.at[from_z, kk])
             for dx in (2, 1, 3):
-                send(gathered.at[kk, came], gathered.at[kk, came], fwd_send, fwd_recv, to_x(around_x[dx]))
+                send(gathered.at[kk, came], gathered.at[kk, came], fwd_send, fwd_recv.at[from_z], to_x(around_x[dx]))
     waits.owe("fwd_send", gathered.at[:, pl.ds(0, 192)], fwd_send)
-    waits.owe("fwd_recv", gathered.at[:, pl.ds(0, 192)], fwd_recv)
+    for i in range(4):
+        waits.owe(("fwd_recv", i), gathered.at[:, pl.ds(0, 48)], fwd_recv.at[near_first[i]])
 
     waits.take(("share_recv", 0))
     for kk in (0, 1):
@@ -213,114 +212,100 @@
         ((target < 128) & (source >= 64) & (source < 67)) | ((target >= 128) & (source >= 67) & (source < 70)), 1.0, 0.0
     ).astype(BF16)
 
-    waits.take("fwd_recv")
-    waits.take("stat_recv")
-
-    table_of = stats[...]
-    moments = jnp.dot(table_of, picks[...], preferred_element_type=F32)
-    for kk in (0, 1):
-        mods = jnp.dot(table_of, fields[kk], preferred_element_type=F32)
-        for part_of in range(3):
-            at = slice(128 * part_of, 128 * part_of + 128)
-            after = slice(384 + 128 * part_of, 512 + 128 * part_of)
-            normed[:, 384 * kk + 128 * part_of : 384 * kk + 128 * part_of + 128] = (
-                (gathered[kk, :, at].astype(F32) - moments[:, 0:128]) * moments[:, 128:256] * (1.0 + mods[:, after])
-                + mods[:, at]
+
+    def of_y(target):
+        return pl.ds(pl.multiple_of(16 * target, 16), 16)
+
+    routes = ((-4, -2), (-3, -1), (3, 1), (-1, -1), (1, 1))
+    for g in range(2):
+        for b in range(2):
+            i = 2 * g + b
+            rows = pl.ds(pl.multiple_of(64 * near_first[i], 64), 64)
+            waits.take(("fwd_recv", i), ("stat_recv", i))
+            lookup = stats[rows, :]
+            moments = jnp.dot(lookup, picks[...], preferred_element_type=F32)
+            for kk in (0, 1):
+                mods = jnp.dot(lookup, fields[kk], preferred_element_type=F32)
+                for part_of in range(3):
+                    at = slice(128 * part_of, 128 * part_of + 128)
+                    after = slice(384 + 128 * part_of, 512 + 128 * part_of)
+                    goal_at = slice(384 * kk + 128 * part_of, 384 * kk + 128 * part_of + 128)
+                    normed[g, 64 * b : 64 * b + 64, goal_at] = (
+                        (gathered[kk, rows, at].astype(F32) - moments[:, 0:128])
+                        * moments[:, 128:256]
+                        * (1.0 + mods[:, after])
+                        + mods[:, at]
+                    ).astype(BF16)
+        if g == 0:
+            waits.take(("share_recv", 1), ("share_recv", 2))
+        part[g] = jnp.dot(normed[g], w1[...], preferred_element_type=F32).astype(BF16)
+        for slot, (goal, via) in enumerate(routes):
+            send(part.at[g, of_y(at_y(goal, g))], part_in.at[g, slot], part_send, part_recv.at[g, slot], to_y(at_y(via, g)))
+            waits.owe(("part", g, slot), part_in.at[g, slot], part_recv.at[g, slot])
+    for g in range(2):
+        waits.take(("part", g, 2))
+        relay[g, 1] = (part[g, of_y(at_y(2, g)), :].astype(F32) + part_in[g, 2].astype(F32)).astype(BF16)
+        send(relay.at[g, 1], part_in.at[g, 6], part_send, part_recv.at[g, 6], to_y(at_y(2, g)))
+        waits.take(("part", g, 1), ("part", g, 0))
+        relay[g, 0] = (
+            part[g, of_y(at_y(-2, g)), :].astype(F32) + part_in[g, 1].astype(F32) + part_in[g, 0].astype(F32)
+        ).astype(BF16)
+        send(relay.at[g, 0], part_in.at[g, 5], part_send, part_recv.at[g, 5], to_y(at_y(-2, g)))
+        waits.owe(("part", g, 5), part_in.at[g, 5], part_recv.at[g, 5])
+        waits.owe(("part", g, 6), part_in.at[g, 6], part_recv.at[g, 6])
+    waits.owe("part_send", part_in, part_send)
+    mine = of_y(y)
+    for g in range(2):
+        waits.take(("part", g, 3), ("part", g, 4), ("part", g, 6), ("part", g, 5))
+        gate_up = part[g, mine, :].astype(F32) + jnp.sum(part_in[g, 3:7].astype(F32), axis=0)
+        gate, up = gate_up[:, 0:512], gate_up[:, 512:1024]
+        hidden[g, mine, :] = (gate / (1.0 + jnp.exp(-gate)) * up).astype(BF16)
+        for dy in far_y[:-1]:
+            send(hidden.at[g, mine], hidden.at[g, mine], hid_send, hid_recv.at[g], to_y(around_y[dy]))
+        waits.owe(("hidden", g), hidden.at[0, pl.ds(0, 112)], hid_recv.at[g])
+    waits.owe("hid_send", hidden.at[:, pl.ds(0, 112)], hid_send)
+    waits.take("sum_send", "tok_send", "fwd_send", "stat_send", "share_send", "part_send")
+    waits.take(("share_recv", 3))
+
+    for g in range(2):
+        waits.take(("hidden", g))
+        for kk in (0, 1):
+            share = jnp.dot(hidden[g], w2[kk], preferred_element_type=F32).astype(BF16)
+            for b in range(2):
+                for goal_x in range(NX):
+                    at = 64 * b + 16 * goal_x
+                    down[2 * g + b, goal_x, kk] = share[at : at + 16, :]
+        for i in (2 * g + 1, 2 * g):
+            for dx in (2, 1, 3):
+                to = around_x[dx]
+                send(down.at[i, to], down_in.at[i, dx - 1], dx_send, dx_recv.at[i], to_x(to))
+            waits.owe(("down", i), down_in.at[i], dx_recv.at[i])
+    waits.owe("dx_send", down_in, dx_send)
+    for i in (1, 0, 3, 2):
+        waits.take(("down", i))
+        for kk in (0, 1):
+            down_mid[i, kk] = (
+                down[i, x, kk].astype(F32) + jnp.sum(down_in[i, :, kk].astype(F32), axis=0)
             ).astype(BF16)
-
-    def of_y(target):
-        return pl.ds(pl.multiple_of(32 * target, 32), 32)
-
-    routes = ((-4, -2), (-3, -1), (3, 1), (-1, -1), (1, 1))
-
-    def send_part(n, slot):
-        goal, via = routes[slot]
-        send(part.at[n, of_y(at_y(goal))], part_in.at[n, slot], part_send, part_recv.at[n, slot], to_y(at_y(via)))
-        waits.owe(("part", n, slot), part_in.at[n, slot], part_recv.at[n, slot])
-
-    for n in range(2):
-        waits.take(("share_recv", 1 + n))
-        at = slice(512 * n, 512 * n + 512)
-        part[n] = jnp.dot(normed[...], w1[:, at], preferred_element_type=F32).astype(BF16)
-        for slot in (0, 1, 2):
-            send_part(n, slot)
-    for n in range(2):
-        for slot in (3, 4):
-            send_part(n, slot)
-    for n in range(2):
-        waits.take(("part", n, 2))
-        relay[n, 1] = (part[n, of_y(at_y(2)), :].astype(F32) + part_in[n, 2].astype(F32)).astype(BF16)
-        send(relay.at[n, 1], part_in.at[n, 6], part_send, part_recv.at[n, 6], to_y(at_y(2)))
-        waits.take(("part", n, 1), ("part", n, 0))
-        relay[n, 0] = (
-            part[n, of_y(at_y(-2)), :].astype(F32) + part_in[n, 1].astype(F32) + part_in[n, 0].astype(F32)
-        ).astype(BF16)
-        send(relay.at[n, 0], part_in.at[n, 5], part_send, part_recv.at[n, 5], to_y(at_y(-2)))
-        waits.owe(("part", n, 5), part_in.at[n, 5], part_recv.at[n, 5])
-        waits.owe(("part", n, 6), part_in.at[n, 6], part_recv.at[n, 6])
-    waits.owe("part_send", part_in, part_send)
-    waits.take("sum_send", "tok_send", "fwd_send", "stat_send", "share_send")
-    waits.take(("share_recv", 3))
-    for n in range(2):
-        waits.take(("part", n, 3), ("part", n, 4), ("part", n, 6), ("part", n, 5))
-
-    mine = of_y(y)
-    gate, up = (part[n, mine, :].astype(F32) + jnp.sum(part_in[n, 3:7].astype(F32), axis=0) for n in range(2))
-    hidden[mine, :] = (gate / (1.0 + jnp.exp(-gate)) * up).astype(BF16)
-    for slot, step in enumerate((2, -2, 1, -1)):
-        send(hidden.at[mine], hidden.at[mine], hid_send, hid_recv.at[min(slot, 2)], to_y(at_y(step)))
-    waits.owe("hid_a", hidden.at[pl.ds(0, 32)], hid_recv.at[0])
-    waits.owe("hid_b", hidden.at[pl.ds(0, 32)], hid_recv.at[1])
-    waits.take("part_send")
-    waits.take("hid_a")
-    came = of_y(at_y(-2))
-    send(hidden.at[came], hidden.at[came], hid_send, hid_recv.at[2], to_y(at_y(2)))
-    send(hidden.at[came], hidden.at[came], hid_send, hid_recv.at[2], to_y(at_y(1)))
-    waits.take("hid_b")
-    came = of_y(at_y(2))
-    send(hidden.at[came], hidden.at[came], hid_send, hid_recv.at[2], to_y(at_y(-1)))
-    waits.owe("hid_send", hidden.at[pl.ds(0, 224)], hid_send)
-    waits.owe("hid_rest", hidden.at[pl.ds(0, 160)], hid_recv.at[2])
-    waits.take("hid_rest")
-
-    for kk in (0, 1):
-        share = jnp.dot(hidden[...], w2[kk], preferred_element_type=F32).astype(BF16)
-        for to_z in range(4):
-            for goal_x in range(NX):
-                at = 64 * to_z + 16 * goal_x
-                down[to_z, goal_x, kk] = share[at : at + 16, :]
-    far_first = near_first[::-1]
-    for i, to_z in enumerate(far_first):
-        send(down.at[to_z, at_x(2)], down_in.at[i, 0], dx_send, dx_recv.at[i, 0], to_x(at_x(-1)))
-        send(down.at[to_z, at_x(1)], down_in.at[i, 1], dx_send, dx_recv.at[i, 1], to_x(at_x(1)))
-    waits.take("hid_send")
-    for i, to_z in enumerate(far_first):
-        await_bytes(down_in.at[i, 0], dx_recv.at[i, 0])
-        down_relay[i] = (down[to_z, at_x(-1)].astype(F32) + down_in[i, 0].astype(F32)).astype(BF16)
-        send(down_relay.at[i], down_in.at[i, 2], dx_send, dx_recv.at[i, 2], to_x(at_x(-1)))
-    for i, to_z in enumerate(far_first):
-        await_bytes(down_in.at[i, 1], dx_recv.at[i, 1])
-        await_bytes(down_in.at[i, 2], dx_recv.at[i, 2])
-        down_mid[i] = (down[to_z, x].astype(F32) + down_in[i, 1].astype(F32) + down_in[i, 2].astype(F32)).astype(BF16)
-        if i < 3:
+        goal = 4 * k + near_first[i]
+        if i:
             for core in (0, 1):
-                send(down_mid.at[i, core], branch_in.at[z], dz_send, dz_recv, place(y, core, 4 * k + to_z, x))
-
-    send(down_mid.at[3, 1 - k], branch_in.at[z], dz_send, dz_recv, place(y, 1 - k, 4 * k + far_first[3], x))
-
-    @pl.when(k == hz)
-    def _():
-        pltpu.make_async_copy(down_mid.at[3, k], branch_in.at[z], dz_recv).start()
-
-    @pl.when(k != hz)
-    def _():
-        send(down_mid.at[3, k], branch_in.at[z], dz_send, dz_recv, place(y, k, 4 * k + far_first[3], x))
-
-    waits.owe("dx_send", down_in, dx_send)
+                send(down_mid.at[i, core], branch_in.at[z], dz_send, dz_recv, place(y, core, goal, x))
+        else:
+            send(down_mid.at[0, 1 - k], branch_in.at[z], dz_send, dz_recv, place(y, 1 - k, goal, x))
+
+            @pl.when(k == hz)
+            def _():
+                pltpu.make_async_copy(down_mid.at[0, k], branch_in.at[z], dz_recv).start()
+
+            @pl.when(k != hz)
+            def _(goal=goal):
+                send(down_mid.at[0, k], branch_in.at[z], dz_send, dz_recv, place(y, k, goal, x))
+
     waits.owe("dz_recv", branch_in, dz_recv)
     waits.owe("dz_send", branch_in.at[pl.ds(0, 7)], dz_send)
     waits.owe("dz_send", own, dz_send, k != hz)
-    waits.take("dz_recv")
+    waits.take("hid_send", "dz_recv")
     branch = jnp.sum(branch_in[...].astype(F32), axis=0)
     out[...] = (own[...].astype(F32) + gate_mod * branch).astype(BF16)
     waits.take("dx_send", "dz_send")
@@ -346,14 +331,13 @@
             vmem((2, 256, 384), BF16),
             vmem((2, 128, 768), BF16),
             vmem((128, 256), BF16),
-            vmem((256, 768), BF16),
-            vmem((2, 256, 512), BF16),
-            vmem((2, 7, 32, 512), BF16),
-            vmem((2, 2, 32, 512), BF16),
-            vmem((256, 512), BF16),
+            vmem((2, 128, 768), BF16),
+            vmem((2, 128, 1024), BF16),
+            vmem((2, 7, 16, 1024), BF16),
+            vmem((2, 2, 16, 1024), BF16),
+            vmem((2, 128, 512), BF16),
             vmem((4, 4, 2, 16, 384), BF16),
             vmem((4, 3, 2, 16, 384), BF16),
-            vmem((4, 2, 16, 384), BF16),
             vmem((4, 2, 16, 384), BF16),
             vmem((8, 16, 384), BF16),
             pltpu.SMEM((2, 16), jnp.int32),
@@ -365,15 +349,15 @@
             dma,
             dma((4, 2)),
             dma,
-            dma,
-            dma,
-            dma,
+            dma((4,)),
+            dma,
+            dma((4,)),
             dma,
             dma((2, 7)),
             dma,
-            dma((3,)),
-            dma,
-            dma((4, 3)),
+            dma((2,)),
+            dma,
+            dma((4,)),
             dma,
             dma,
         ],

time: 60.9 us -> 56.3 us (0.924)
  Pallas kernels: 59.3 us -> 54.7 us
    pallas_call x1, Pallas kernels: 59.3 us -> 54.7 us  [on_device(): pl.pallas_call(kernel, out_shape=jax.ShapeDtypeStruct((16, 384), BF16), i...]
where the time goes in v5:
time: 56.3 us; the launch traced here: 56.1 us
  Pallas kernels  54.7 us (97%)
  local copies, waits for them, and re-layouts  1.31 us (2%)
    pallas_call x1, Pallas kernels, on_device(): pl.pallas_call(kernel, out_shape=jax.ShapeDtypeStruct((16, 384), BF16), i...  54.7 us
    unnamed x1, local copies, waits for them, and re-layouts  1.31 us

profile of v5, /device:TPU:1, one launch (start us, length us, event | category | flops | bytes accessed | tf_op | source)
XLA Modules:
  0.0 56.1 jit_solution(14704640860699212142)
XLA Ops:
  0.0 54.7 %modulated_feed_forward.1 = bf16[16,384]{1,0:T(8,128)(2,1)} custom-call(bf16[16,384]{1,0:T(8,128)(2,1)} %tokens.1, s32[16]{0:T(128)} %frame.1, s32[16]{0:T(128)} %noise.1, bf16[3,64,384]{2,1,0:T(8,128)(2,1)} %bitcast.1, bf16[384,512]{1,0:T(8,128)(2,1)} %gate_w.1, bf16[384,512]{1,0:T(8,128)(2,1)} %up_w.1, bf16[512,384]{1,0:T(8,128)(2,1)} %down_w.1), custom_call_target="tpu_custom_call" | custom-call | flops 604000000 | bytes 1400000 | tf_op jit(solution)/shard_map/modulated_feed_forward/pallas_call | solution.py:317
  54.7 1.3 %copy.9 = bf16[16,384]{1,0:T(8,128)(2,1)} copy(bf16[16,384]{1,0:T(8,128)(2,1)} %modulated_feed_forward.1) | data formatting | bytes 24576

commit v6 on v5

--- a/solution.py
+++ b/solution.py
@@ -61,7 +61,7 @@
     normed, part, part_in, relay, hidden, down, down_in, down_mid, branch_in, levels,
     local_sem, share_send, share_recv, sum_send, sum_recv, tok_send, tok_recv,
     fwd_send, fwd_recv, stat_send, stat_recv, part_send, part_recv, hid_send, hid_recv,
-    dx_send, dx_recv, dz_send, dz_recv,
+    dx_send, dx_recv, dz_send, dz_recv, ready,
 ):
     row, col = lax.axis_index("row"), lax.axis_index("col")
     y, k, z, x = row // 2, row % 2, col // NX, col % NX
@@ -98,18 +98,25 @@
     for copy in small:
         copy.start()
     barrier = pltpu.get_barrier_semaphore()
-    peers = [place(y, core, around_z[dz], x) for dz in far_z for core in (k, 1 - k)]
-    peers += [place(around_y[dy], core, z, x) for dy in far_y for core in (k, 1 - k)][:-2] + [sibling]
-    peers += [to_x(around_x[dx]) for dx in (2, 1, 3)]
-    for peer in peers:
-        pl.semaphore_signal(barrier, inc=1, device_id=peer, device_id_type=MESH)
+
+    def enter(device):
+        pl.semaphore_signal(barrier, inc=1, device_id=device, device_id_type=MESH)
+
+    for dz in far_z:
+        enter(place(y, 1, around_z[dz], x))
     for i in range(4):
         from_z = 4 * k + i
 
         @pl.when(from_z != z)
         def _(from_z=from_z):
             for dx in (2, 1, 3):
-                pl.semaphore_signal(barrier, inc=1, device_id=place(y, k, from_z, around_x[dx]), device_id_type=MESH)
+                enter(place(y, 1, from_z, around_x[dx]))
+
+    for dy in far_y[:-1]:
+        enter(place(around_y[dy], 0, z, x))
+    for dx in (2, 1, 3):
+        enter(place(y, 0, z, around_x[dx]))
+    enter(sibling)
 
     own_copy.wait()
     wide = own[...].astype(F32)
@@ -123,22 +130,14 @@
     sum_out[0] = sums
     sum_in[row] = sums
 
-    pl.semaphore_wait(barrier, len(peers) + 21 * holds)
-
-    block = pl.ds(64 * zz + 16 * x, 16)
-    for dz in (4, 3, 5, 2, 6, 1, 7):
-        send(own, gathered.at[k, block], tok_send, tok_recv.at[zz, k], place(y, hz, around_z[dz], x))
-
-    @pl.when(k == hz)
-    def _():
-        pltpu.make_async_copy(own, gathered.at[k, block], tok_recv.at[zz, k]).start()
-
-    @pl.when(k != hz)
-    def _():
-        send(own, gathered.at[k, block], tok_send, tok_recv.at[zz, k], sibling)
-
-    waits.owe("tok_send", gathered.at[0, pl.ds(0, 112)], tok_send)
-    waits.owe("tok_send", own, tok_send, k != hz)
+    @pl.when(k == 0)
+    def _():
+        pl.semaphore_wait(barrier, 21)
+        pl.semaphore_signal(ready.at[0], inc=1, device_id=sibling, device_id_type=MESH)
+
+    @pl.when(k == 1)
+    def _():
+        pl.semaphore_wait(ready.at[0], 1)
 
     for dy in far_y:
         for core in (k, 1 - k) if dy else (1 - k,):
@@ -161,6 +160,30 @@
         waits.owe("share_send", like, share_send.at[i])
         waits.owe(("share_recv", i), like, share_recv.at[i])
         waits.owe(("share_recv", i), like, local_sem.at[1 + i])
+
+    @pl.when(k == 1)
+    def _():
+        pl.semaphore_wait(barrier, 36)
+        pl.semaphore_signal(ready.at[1], inc=1, device_id=sibling, device_id_type=MESH)
+
+    @pl.when(k == 0)
+    def _():
+        pl.semaphore_wait(ready.at[1], 1)
+
+    block = pl.ds(64 * zz + 16 * x, 16)
+    for dz in (4, 3, 5, 2, 6, 1, 7):
+        send(own, gathered.at[k, block], tok_send, tok_recv.at[zz, k], place(y, hz, around_z[dz], x))
+
+    @pl.when(k == hz)
+    def _():
+        pltpu.make_async_copy(own, gathered.at[k, block], tok_recv.at[zz, k]).start()
+
+    @pl.when(k != hz)
+    def _():
+        send(own, gathered.at[k, block], tok_send, tok_recv.at[zz, k], sibling)
+
+    waits.owe("tok_send", gathered.at[0, pl.ds(0, 112)], tok_send)
+    waits.owe("tok_send", own, tok_send, k != hz)
 
     for copy in small:
         copy.wait()
@@ -360,6 +383,7 @@
             dma((4,)),
             dma,
             dma,
+            pltpu.SemaphoreType.REGULAR((2,)),
         ],
         compiler_params=pltpu.CompilerParams(
             collective_id=0, has_side_effects=True, vmem_limit_bytes=60 << 20

time: 56.3 us -> 54 us (0.959)
  Pallas kernels: 54.7 us -> 52.4 us
    pallas_call x1, Pallas kernels: 54.7 us -> 52.4 us  [on_device(): pl.pallas_call(kernel, out_shape=jax.ShapeDtypeStruct((16, 384), BF16), i...]
where the time goes in v6:
time: 54 us; the launch traced here: 53.7 us
  Pallas kernels  52.4 us (97%)
  local copies, waits for them, and re-layouts  1.31 us (2%)
    pallas_call x1, Pallas kernels, on_device(): pl.pallas_call(kernel, out_shape=jax.ShapeDtypeStruct((16, 384), BF16), i...  52.4 us
    unnamed x1, local copies, waits for them, and re-layouts  1.31 us

profile of v6, /device:TPU:1, one launch (start us, length us, event | category | flops | bytes accessed | tf_op | source)
XLA Modules:
  0.0 53.7 jit_solution(1407199813393195881)
XLA Ops:
  0.0 52.4 %modulated_feed_forward.1 = bf16[16,384]{1,0:T(8,128)(2,1)} custom-call(bf16[16,384]{1,0:T(8,128)(2,1)} %tokens.1, s32[16]{0:T(128)} %frame.1, s32[16]{0:T(128)} %noise.1, bf16[3,64,384]{2,1,0:T(8,128)(2,1)} %bitcast.1, bf16[384,512]{1,0:T(8,128)(2,1)} %gate_w.1, bf16[384,512]{1,0:T(8,128)(2,1)} %up_w.1, bf16[512,384]{1,0:T(8,128)(2,1)} %down_w.1), custom_call_target="tpu_custom_call" | custom-call | flops 604000000 | bytes 1400000 | tf_op jit(solution)/shard_map/modulated_feed_forward/pallas_call | solution.py:340
  52.4 1.3 %copy.9 = bf16[16,384]{1,0:T(8,128)(2,1)} copy(bf16[16,384]{1,0:T(8,128)(2,1)} %modulated_feed_forward.1) | data formatting | bytes 24576

commit v7 on v6

--- a/solution.py
+++ b/solution.py
@@ -1,3 +1,5 @@
+import functools
+
 import jax
 import jax.numpy as jnp
 from jax import lax
@@ -60,7 +62,7 @@
     own, table, w1, w2, sum_out, sum_in, stat_out, stats, gathered, fields, picks,
     normed, part, part_in, relay, hidden, down, down_in, down_mid, branch_in, levels,
     local_sem, share_send, share_recv, sum_send, sum_recv, tok_send, tok_recv,
-    fwd_send, fwd_recv, stat_send, stat_recv, part_send, part_recv, hid_send, hid_recv,
+    fwd_send, fwd_recv, stat_send, stat_recv, statf_recv, part_send, part_recv, hid_send, hid_recv,
     dx_send, dx_recv, dz_send, dz_recv, ready,
 ):
     row, col = lax.axis_index("row"), lax.axis_index("col")
@@ -84,6 +86,7 @@
     outward = [zz, 1 - zz + 4 * upper, 2 - upper, 3 - 3 * upper]
     holds = 1 - (k - hz) * (k - hz)
     near_first = [outward[i] * holds + outward[3 - i] * (1 - holds) for i in range(4)]
+    order = [i * (1 - k) + near_first[i] * k for i in range(4)]
     around_z = {dz: lax.rem(z + dz, NZ) for dz in range(1, NZ)}
     around_y = {dy: lax.rem(y + dy, NY) for dy in range(NY)}
     around_x = {dx: lax.rem(x + dx, NX) for dx in range(1, NX)}
@@ -104,13 +107,14 @@
 
     for dz in far_z:
         enter(place(y, 1, around_z[dz], x))
-    for i in range(4):
-        from_z = 4 * k + i
-
-        @pl.when(from_z != z)
-        def _(from_z=from_z):
-            for dx in (2, 1, 3):
-                enter(place(y, 1, from_z, around_x[dx]))
+    @pl.when(k == 1)
+    def _():
+        for from_z in range(4, NZ):
+
+            @pl.when(from_z != z)
+            def _(from_z=from_z):
+                for dx in (2, 1, 3):
+                    enter(place(y, 1, from_z, around_x[dx]))
 
     for dy in far_y[:-1]:
         enter(place(around_y[dy], 0, z, x))
@@ -147,23 +151,27 @@
 
     half = w1.at[pl.ds(0, 384), pl.ds(0, 512)]
     rows = pl.ds(384 * k, 384)
-    for i, (source, goal, like) in enumerate(
-        (
-            (modulation, table.at[k], table.at[0]),
-            (gate_w, w1.at[rows, pl.ds(0, 512)], half),
-            (up_w, w1.at[rows, pl.ds(512, 512)], half),
-            (down_w, w2.at[k], w2.at[0]),
-        )
-    ):
-        pltpu.make_async_copy(source, goal, local_sem.at[1 + i]).start()
-        send(source, goal, share_send.at[i], share_recv.at[i], sibling)
+    shared = (
+        (modulation, table.at[k], table.at[0]),
+        (gate_w, w1.at[rows, pl.ds(0, 512)], half),
+        (up_w, w1.at[rows, pl.ds(512, 512)], half),
+        (down_w, w2.at[k], w2.at[0]),
+    )
+    for i, (_, _, like) in enumerate(shared):
         waits.owe("share_send", like, share_send.at[i])
         waits.owe(("share_recv", i), like, share_recv.at[i])
         waits.owe(("share_recv", i), like, local_sem.at[1 + i])
 
+    def share():
+        for i, (source, goal, _) in enumerate(shared):
+            pltpu.make_async_copy(source, goal, local_sem.at[1 + i]).start()
+            send(source, goal, share_send.at[i], share_recv.at[i], sibling)
+
+    pl.when(hz == 0)(share)
+
     @pl.when(k == 1)
     def _():
-        pl.semaphore_wait(barrier, 36)
+        pl.semaphore_wait(barrier, 15 + 21 * hz)
         pl.semaphore_signal(ready.at[1], inc=1, device_id=sibling, device_id_type=MESH)
 
     @pl.when(k == 0)
@@ -171,8 +179,8 @@
         pl.semaphore_wait(ready.at[1], 1)
 
     block = pl.ds(64 * zz + 16 * x, 16)
-    for dz in (4, 3, 5, 2, 6, 1, 7):
-        send(own, gathered.at[k, block], tok_send, tok_recv.at[zz, k], place(y, hz, around_z[dz], x))
+    for to_z in [4 * (1 - hz) + lax.rem(zz + d, 4) for d in (0, 1, 3, 2)] + [4 * hz + lax.rem(zz + d, 4) for d in (2, 1, 3)]:
+        send(own, gathered.at[k, block], tok_send, tok_recv.at[zz, k], place(y, hz, to_z, x))
 
     @pl.when(k == hz)
     def _():
@@ -185,6 +193,7 @@
     waits.owe("tok_send", gathered.at[0, pl.ds(0, 112)], tok_send)
     waits.owe("tok_send", own, tok_send, k != hz)
 
+    pl.when(hz == 1)(share)
     for copy in small:
         copy.wait()
     onehot = zero
@@ -199,7 +208,7 @@
     scale = lax.rsqrt(square - center * center + EPS)
     stat_out[...] = in_lanes(lane, 64, pieces(center) + pieces(scale), onehot).astype(BF16)
 
-    @pl.when(k == hz)
+    @pl.when((k == 1) & (hz == 1))
     def _():
         for dz in far_z:
             for to in (around_x[2], around_x[1], around_x[3], x):
@@ -208,20 +217,40 @@
             send(stat_out, stats.at[block], stat_send, stat_recv.at[zz], to_x(around_x[dx]))
         pltpu.make_async_copy(stat_out, stats.at[block], stat_recv.at[zz]).start()
 
-    waits.owe("stat_send", stats.at[pl.ds(0, 240)], stat_send, k == hz)
-    waits.owe("stat_send", stats, stat_send, k == hz)
+    @pl.when((k == 0) & (hz == 0))
+    def _():
+        for dz in far_z:
+            send(stat_out, stats.at[block], stat_send, stat_recv.at[zz], place(y, k, around_z[dz], x))
+        pltpu.make_async_copy(stat_out, stats.at[block], stat_recv.at[zz]).start()
+
+    waits.owe("stat_send", stats, stat_send, (k == 1) & (hz == 1))
+    waits.owe("stat_send", stats.at[pl.ds(0, 240)], stat_send, (k == 1) & (hz == 1))
+    waits.owe("stat_send", stats.at[pl.ds(0, 112)], stat_send, (k == 0) & (hz == 0))
+    waits.owe("stat_send", stats.at[pl.ds(0, 192)], stat_send, k == 0)
+
+    def forward(like, from_z, send_sem, recv_sem):
+        for dx in (2, 1, 3):
+            send(like, like, send_sem, recv_sem.at[from_z], to_x(around_x[dx]))
+
+    def forward_stats(from_z):
+        came = stats.at[pl.ds(64 * from_z + 16 * x, 16)]
+        await_bytes(came, stat_recv.at[from_z])
+        forward(came, from_z, stat_send, statf_recv)
+
+    for i, from_z in enumerate(near_first):
+        for kk in (0, 1):
+            came = gathered.at[kk, pl.ds(64 * from_z + 16 * x, 16)]
+            await_bytes(came, tok_recv.at[from_z, kk])
+            forward(came, from_z, fwd_send, fwd_recv)
+        if i % 2:
+            for near in near_first[i - 1 : i + 1]:
+                pl.when(k == 0)(functools.partial(forward_stats, near))
     for i in range(4):
-        waits.owe(("stat_recv", i), stats.at[pl.ds(0, 64)], stat_recv.at[near_first[i]])
-
-    for from_z in near_first:
-        came = pl.ds(64 * from_z + 16 * x, 16)
-        for kk in (0, 1):
-            await_bytes(gathered.at[kk, came], tok_recv.at[from_z, kk])
-            for dx in (2, 1, 3):
-                send(gathered.at[kk, came], gathered.at[kk, came], fwd_send, fwd_recv.at[from_z], to_x(around_x[dx]))
+        waits.owe(("stat_recv", i), stats.at[pl.ds(0, 48)], statf_recv.at[order[i]], k == 0)
+        waits.owe(("stat_recv", i), stats.at[pl.ds(0, 64)], stat_recv.at[order[i]], k == 1)
     waits.owe("fwd_send", gathered.at[:, pl.ds(0, 192)], fwd_send)
     for i in range(4):
-        waits.owe(("fwd_recv", i), gathered.at[:, pl.ds(0, 48)], fwd_recv.at[near_first[i]])
+        waits.owe(("fwd_recv", i), gathered.at[:, pl.ds(0, 48)], fwd_recv.at[order[i]])
 
     waits.take(("share_recv", 0))
     for kk in (0, 1):
@@ -243,7 +272,7 @@
     for g in range(2):
         for b in range(2):
             i = 2 * g + b
-            rows = pl.ds(pl.multiple_of(64 * near_first[i], 64), 64)
+            rows = pl.ds(pl.multiple_of(64 * order[i], 64), 64)
             waits.take(("fwd_recv", i), ("stat_recv", i))
             lookup = stats[rows, :]
             moments = jnp.dot(lookup, picks[...], preferred_element_type=F32)
@@ -298,32 +327,28 @@
                 for goal_x in range(NX):
                     at = 64 * b + 16 * goal_x
                     down[2 * g + b, goal_x, kk] = share[at : at + 16, :]
-        for i in (2 * g + 1, 2 * g):
+        for i in (2 * g, 2 * g + 1):
             for dx in (2, 1, 3):
                 to = around_x[dx]
                 send(down.at[i, to], down_in.at[i, dx - 1], dx_send, dx_recv.at[i], to_x(to))
             waits.owe(("down", i), down_in.at[i], dx_recv.at[i])
     waits.owe("dx_send", down_in, dx_send)
-    for i in (1, 0, 3, 2):
+    for i in range(4):
         waits.take(("down", i))
         for kk in (0, 1):
             down_mid[i, kk] = (
                 down[i, x, kk].astype(F32) + jnp.sum(down_in[i, :, kk].astype(F32), axis=0)
             ).astype(BF16)
-        goal = 4 * k + near_first[i]
-        if i:
-            for core in (0, 1):
-                send(down_mid.at[i, core], branch_in.at[z], dz_send, dz_recv, place(y, core, goal, x))
-        else:
-            send(down_mid.at[0, 1 - k], branch_in.at[z], dz_send, dz_recv, place(y, 1 - k, goal, x))
-
-            @pl.when(k == hz)
-            def _():
-                pltpu.make_async_copy(down_mid.at[0, k], branch_in.at[z], dz_recv).start()
-
-            @pl.when(k != hz)
-            def _(goal=goal):
-                send(down_mid.at[0, k], branch_in.at[z], dz_send, dz_recv, place(y, k, goal, x))
+        goal = 4 * k + order[i]
+        send(down_mid.at[i, 1 - k], branch_in.at[z], dz_send, dz_recv, place(y, 1 - k, goal, x))
+
+        @pl.when(goal == z)
+        def _(i=i):
+            pltpu.make_async_copy(down_mid.at[i, k], branch_in.at[z], dz_recv).start()
+
+        @pl.when(goal != z)
+        def _(i=i, goal=goal):
+            send(down_mid.at[i, k], branch_in.at[z], dz_send, dz_recv, place(y, k, goal, x))
 
     waits.owe("dz_recv", branch_in, dz_recv)
     waits.owe("dz_send", branch_in.at[pl.ds(0, 7)], dz_send)
@@ -375,6 +400,7 @@
             dma((4,)),
             dma,
             dma((4,)),
+            dma((4,)),
             dma,
             dma((2, 7)),
             dma,

time: 54 us -> 53.1 us (0.983)
  Pallas kernels: 52.4 us -> 51.5 us
    pallas_call x1, Pallas kernels: 52.4 us -> 51.5 us  [on_device(): pl.pallas_call(kernel, out_shape=jax.ShapeDtypeStruct((16, 384), BF16), i...]
where the time goes in v7:
time: 53.1 us; the launch traced here: 52.8 us
  Pallas kernels  51.5 us (97%)
  local copies, waits for them, and re-layouts  1.31 us (2%)
    pallas_call x1, Pallas kernels, on_device(): pl.pallas_call(kernel, out_shape=jax.ShapeDtypeStruct((16, 384), BF16), i...  51.5 us
    unnamed x1, local copies, waits for them, and re-layouts  1.31 us

profile of v7, /device:TPU:1, one launch (start us, length us, event | category | flops | bytes accessed | tf_op | source)
XLA Modules:
  0.0 52.8 jit_solution(14678261453929689192)
XLA Ops:
  0.0 51.5 %modulated_feed_forward.1 = bf16[16,384]{1,0:T(8,128)(2,1)} custom-call(bf16[16,384]{1,0:T(8,128)(2,1)} %tokens.1, s32[16]{0:T(128)} %frame.1, s32[16]{0:T(128)} %noise.1, bf16[3,64,384]{2,1,0:T(8,128)(2,1)} %bitcast.1, bf16[384,512]{1,0:T(8,128)(2,1)} %gate_w.1, bf16[384,512]{1,0:T(8,128)(2,1)} %up_w.1, bf16[512,384]{1,0:T(8,128)(2,1)} %down_w.1), custom_call_target="tpu_custom_call" | custom-call | flops 604000000 | bytes 1400000 | tf_op jit(solution)/shard_map/modulated_feed_forward/pallas_call | solution.py:365
  51.5 1.3 %copy.9 = bf16[16,384]{1,0:T(8,128)(2,1)} copy(bf16[16,384]{1,0:T(8,128)(2,1)} %modulated_feed_forward.1) | data formatting | bytes 24576

commit v8 on v7

--- a/solution.py
+++ b/solution.py
@@ -237,13 +237,13 @@
         await_bytes(came, stat_recv.at[from_z])
         forward(came, from_z, stat_send, statf_recv)
 
-    for i, from_z in enumerate(near_first):
+    for i, from_z in enumerate(order):
         for kk in (0, 1):
             came = gathered.at[kk, pl.ds(64 * from_z + 16 * x, 16)]
             await_bytes(came, tok_recv.at[from_z, kk])
             forward(came, from_z, fwd_send, fwd_recv)
         if i % 2:
-            for near in near_first[i - 1 : i + 1]:
+            for near in order[i - 1 : i + 1]:
                 pl.when(k == 0)(functools.partial(forward_stats, near))
     for i in range(4):
         waits.owe(("stat_recv", i), stats.at[pl.ds(0, 48)], statf_recv.at[order[i]], k == 0)

time: 53.1 us -> 51.9 us (0.977)
  Pallas kernels: 51.5 us -> 50.3 us
    pallas_call x1, Pallas kernels: 51.5 us -> 50.3 us  [on_device(): pl.pallas_call(kernel, out_shape=jax.ShapeDtypeStruct((16, 384), BF16), i...]
where the time goes in v8:
time: 51.9 us; the launch traced here: 51.6 us
  Pallas kernels  50.3 us (97%)
  local copies, waits for them, and re-layouts  1.31 us (3%)
    pallas_call x1, Pallas kernels, on_device(): pl.pallas_call(kernel, out_shape=jax.ShapeDtypeStruct((16, 384), BF16), i...  50.3 us
    unnamed x1, local copies, waits for them, and re-layouts  1.31 us

profile of v8, /device:TPU:1, one launch (start us, length us, event | category | flops | bytes accessed | tf_op | source)
XLA Modules:
  0.0 51.6 jit_solution(2921553183206832213)
XLA Ops:
  0.0 50.3 %modulated_feed_forward.1 = bf16[16,384]{1,0:T(8,128)(2,1)} custom-call(bf16[16,384]{1,0:T(8,128)(2,1)} %tokens.1, s32[16]{0:T(128)} %frame.1, s32[16]{0:T(128)} %noise.1, bf16[3,64,384]{2,1,0:T(8,128)(2,1)} %bitcast.1, bf16[384,512]{1,0:T(8,128)(2,1)} %gate_w.1, bf16[384,512]{1,0:T(8,128)(2,1)} %up_w.1, bf16[512,384]{1,0:T(8,128)(2,1)} %down_w.1), custom_call_target="tpu_custom_call" | custom-call | flops 604000000 | bytes 1400000 | tf_op jit(solution)/shard_map/modulated_feed_forward/pallas_call | solution.py:365
  50.3 1.3 %copy.9 = bf16[16,384]{1,0:T(8,128)(2,1)} copy(bf16[16,384]{1,0:T(8,128)(2,1)} %modulated_feed_forward.1) | data formatting | bytes 24576

commit v9 on v8

--- a/solution.py
+++ b/solution.py
@@ -86,7 +86,7 @@
     outward = [zz, 1 - zz + 4 * upper, 2 - upper, 3 - 3 * upper]
     holds = 1 - (k - hz) * (k - hz)
     near_first = [outward[i] * holds + outward[3 - i] * (1 - holds) for i in range(4)]
-    order = [i * (1 - k) + near_first[i] * k for i in range(4)]
+    order = [i * (1 - k) + (3 - i) * k for i in range(4)]
     around_z = {dz: lax.rem(z + dz, NZ) for dz in range(1, NZ)}
     around_y = {dy: lax.rem(y + dy, NY) for dy in range(NY)}
     around_x = {dx: lax.rem(x + dx, NX) for dx in range(1, NX)}

time: 51.9 us -> 52.3 us (level)
  no operation moved by 1% of the time
where the time goes in v9:
time: 52.3 us; the launch traced here: 52.1 us
  Pallas kernels  50.8 us (97%)
  local copies, waits for them, and re-layouts  1.31 us (3%)
    pallas_call x1, Pallas kernels, on_device(): pl.pallas_call(kernel, out_shape=jax.ShapeDtypeStruct((16, 384), BF16), i...  50.8 us
    unnamed x1, local copies, waits for them, and re-layouts  1.31 us

profile of v9, /device:TPU:1, one launch (start us, length us, event | category | flops | bytes accessed | tf_op | source)
XLA Modules:
  0.0 52.1 jit_solution(1890664202388080390)
XLA Ops:
  0.0 50.8 %modulated_feed_forward.1 = bf16[16,384]{1,0:T(8,128)(2,1)} custom-call(bf16[16,384]{1,0:T(8,128)(2,1)} %tokens.1, s32[16]{0:T(128)} %frame.1, s32[16]{0:T(128)} %noise.1, bf16[3,64,384]{2,1,0:T(8,128)(2,1)} %bitcast.1, bf16[384,512]{1,0:T(8,128)(2,1)} %gate_w.1, bf16[384,512]{1,0:T(8,128)(2,1)} %up_w.1, bf16[512,384]{1,0:T(8,128)(2,1)} %down_w.1), custom_call_target="tpu_custom_call" | custom-call | flops 604000000 | bytes 1400000 | tf_op jit(solution)/shard_map/modulated_feed_forward/pallas_call | solution.py:365
  50.8 1.3 %copy.9 = bf16[16,384]{1,0:T(8,128)(2,1)} copy(bf16[16,384]{1,0:T(8,128)(2,1)} %modulated_feed_forward.1) | data formatting | bytes 24576
